TPU v7x, 32 devices: a whole 2x2x4 slice. The times are simulated.
32 devices in a mesh: head: 2 (over y), blk: 16 (over z, x, core).
Axes of the slice: x: 2, y: 2, z: 4, core: 2. Of those that a mesh axis runs over, the one named last changes fastest.
Arguments:
- tokens: bfloat16 [8192, 768], P(('blk', 'head')), may hold values from -6 to 6
- w_qkv: bfloat16 [768, 2304], P(('blk', 'head')), may hold values from -0.21875 to 0.21875
- w_out: bfloat16 [768, 768], P(('blk', 'head')), may hold values from -1.5 to 1.5
- w_ff1: bfloat16 [768, 3072], P(('blk', 'head')), may hold values from -0.21875 to 0.21875
- w_ff2: bfloat16 [3072, 768], P(('blk', 'head')), may hold values from -0.109375 to 0.109375
- norm_gains: bfloat16 [2, 768], P(None, ('blk', 'head')), may hold values from 0.5 to 1.5
- norm_biases: bfloat16 [2, 768], P(None, ('blk', 'head')), may hold values from -4 to 4
- proj_biases: bfloat16 [4, 768], P(None, ('blk', 'head')), may hold values from -2 to 2
- ff_bias: bfloat16 [3072], P(('blk', 'head')), may hold values from -6 to 6
- doc_starts: int32 [33], replicated, may hold values from 1 to 8192, as said below
- d_out: bfloat16 [8192, 768], P(('blk', 'head')), may hold values from -6 to 6
Outputs:
- out: bfloat16 [8192, 768], P(('blk', 'head'))
- d_tokens: bfloat16 [8192, 768], P(('blk', 'head'))
- g_qkv: float32 [768, 2304], P(('blk', 'head'))
- g_out: float32 [768, 768], P(('blk', 'head'))
- g_ff1: float32 [768, 3072], P(('blk', 'head'))
- g_ff2: float32 [3072, 768], P(('blk', 'head'))
- g_gains: float32 [2, 768], P(None, ('blk', 'head'))
- g_norm_biases: float32 [2, 768], P(None, ('blk', 'head'))
- g_proj_biases: float32 [4, 768], P(None, ('blk', 'head'))
- g_ff_bias: float32 [3072], P(('blk', 'head'))
Inputs may be any that keep to these rules, and one draw needn't show every extreme that they name: doc_starts[0] is 1 or more and the entries never fall. Each entry below 8192 starts a document that runs to the next larger entry; the last one runs past 8192 on to position doc_starts[0] - 1 of the start. Every document holds 1 to 2048 tokens, and the one that runs past the end holds exactly 2048; entries equal to 8192 start no document.
All inputs are finite; a program needn't handle non-finite values.
Results may differ from a plain program's by a relative error of at most 0.025.
Values may be sent and summed in bfloat16 or wider, within the bound.
A program may use at most 128 MiB of HBM per device.

v0:
```python
import jax
import jax.numpy as jnp
from jax import lax
from jax.sharding import PartitionSpec as P

H = 12
HD = 64
REACH = 4


EPSILON = 1e-06
NEGATIVE = -1e30


def from_behind(value, axis, steps):
    count = lax.axis_size(axis)
    pairs = [(source, (source + steps) % count) for source in range(count)]
    return lax.ppermute(value, axis, pairs)


def norm_rows(values, gain_row, shift_row):
    center = values - jnp.mean(values, axis=-1, keepdims=True)
    spread = jnp.mean(center * center, axis=-1, keepdims=True)
    return center * lax.rsqrt(spread + EPSILON) * gain_row + shift_row


def gelu_exact(values):
    return 0.5 * values * (1.0 + jax.scipy.special.erf(values * 0.7071067811865476))


def doc_index(doc_starts, first_pos, how_many, total_rows):
    places = first_pos + jnp.arange(how_many, dtype=jnp.int32)
    counted = jnp.sum((doc_starts[None, :] <= places[:, None]).astype(jnp.int32), axis=1)
    live = jnp.sum((doc_starts < total_rows).astype(jnp.int32))
    return jnp.mod(counted, live)


def fold_block(softmax_state, query_rows, query_ids, key_rows, value_rows, key_ids, score_scale):
    running, denominator, weighted = softmax_state
    scores = (
        jnp.einsum("qhd,khd->hqk", query_rows, key_rows, preferred_element_type=jnp.float32)
        * score_scale
    )
    allowed = query_ids[:, None] == key_ids[None, :]
    scores = jnp.where(allowed[None, :, :], scores, NEGATIVE)
    highest = jnp.maximum(running, jnp.max(scores, axis=2))
    factor = jnp.exp(running - highest)
    exp_terms = jnp.exp(scores - highest[:, :, None])
    denominator = denominator * factor + jnp.sum(exp_terms, axis=2)
    weighted = weighted * jnp.transpose(factor)[:, :, None] + jnp.einsum(
        "hqk,khd->qhd",
        exp_terms.astype(jnp.bfloat16),
        value_rows,
        preferred_element_type=jnp.float32,
    )
    return (highest, denominator, weighted)


def back_block(
    query_rows, grad_rows, log_sums, deltas, query_ids, key_rows, value_rows, key_ids, score_scale
):
    scores = (
        jnp.einsum("qhd,khd->hqk", query_rows, key_rows, preferred_element_type=jnp.float32)
        * score_scale
    )
    allowed = query_ids[:, None] == key_ids[None, :]
    scores = jnp.where(allowed[None, :, :], scores, NEGATIVE)
    probabilities = jnp.where(allowed[None, :, :], jnp.exp(scores - log_sums[:, :, None]), 0.0)
    grad_probs = jnp.einsum(
        "qhd,khd->hqk", grad_rows, value_rows, preferred_element_type=jnp.float32
    )
    grad_scores = (probabilities * (grad_probs - deltas[:, :, None])).astype(jnp.bfloat16)
    grad_queries = None
    grad_keys = None
    grad_values = None
    grad_queries = (
        jnp.einsum("hqk,khd->qhd", grad_scores, key_rows, preferred_element_type=jnp.float32)
        * score_scale
    )
    grad_values = jnp.einsum(
        "hqk,qhd->khd",
        probabilities.astype(jnp.bfloat16),
        grad_rows,
        preferred_element_type=jnp.float32,
    )
    grad_keys = (
        jnp.einsum("hqk,qhd->khd", grad_scores, query_rows, preferred_element_type=jnp.float32)
        * score_scale
    )
    return (grad_queries, grad_keys, grad_values)


def body(
    tokens,
    w_qkv,
    w_out,
    w_ff1,
    w_ff2,
    norm_gains,
    norm_biases,
    proj_biases,
    ff_bias,
    doc_starts,
    d_out,
):
    gathered = (
        lax.all_gather(w_qkv, ("blk", "head"), axis=0, tiled=True),
        lax.all_gather(w_out, ("blk", "head"), axis=0, tiled=True),
        lax.all_gather(w_ff1, ("blk", "head"), axis=0, tiled=True),
        lax.all_gather(w_ff2, ("blk", "head"), axis=0, tiled=True),
        lax.all_gather(norm_gains, ("blk", "head"), axis=1, tiled=True),
        lax.all_gather(norm_biases, ("blk", "head"), axis=1, tiled=True),
        lax.all_gather(proj_biases, ("blk", "head"), axis=1, tiled=True),
        lax.all_gather(ff_bias, ("blk", "head"), axis=0, tiled=True),
    )
    full_qkv = gathered[0]
    full_out = gathered[1]
    full_ff1 = gathered[2]
    full_ff2 = gathered[3]
    gains_all = gathered[4].astype(jnp.float32)
    shifts_all = gathered[5].astype(jnp.float32)
    biases_all = gathered[6].astype(jnp.float32)
    ff_shift = gathered[7].astype(jnp.float32)
    model_width = full_out.shape[0]
    groups = lax.axis_size("head")
    cycle_size = lax.axis_size("blk")
    tok_rows = tokens.shape[0]
    block_rows = tok_rows * groups
    local_heads = H // groups
    slab_width = model_width // groups
    total_rows = block_rows * cycle_size
    position = lax.axis_index("blk")
    score_scale = HD ** (-0.5)
    span_rows = min(512, block_rows)
    span_count = block_rows // span_rows
    joined = jnp.dot(tokens, full_qkv, preferred_element_type=jnp.float32)
    zero_row = jnp.zeros((model_width,), jnp.float32)
    joined = joined + jnp.concatenate([biases_all[0], zero_row, biases_all[1]])
    packed = joined.astype(jnp.bfloat16).reshape(tok_rows, 3, groups, slab_width)
    by_heads = lax.all_to_all(packed, "head", split_axis=2, concat_axis=0, tiled=True)
    queries = by_heads[:, 0, 0].reshape(block_rows, local_heads, HD)
    own_pair = by_heads[:, 1:, 0]
    query_blocks = queries.reshape(span_count, span_rows, local_heads, HD)
    query_ids = doc_index(doc_starts, position * block_rows, block_rows, total_rows)
    id_blocks = query_ids.reshape(span_count, span_rows)

    def source_ids(source):
        return doc_index(
            doc_starts, jnp.mod(source, cycle_size) * block_rows, block_rows, total_rows
        )

    def meets(other_ids):
        return jnp.any(query_ids[:, None] == other_ids[None, :])

    def visit_block(softmax_state, pair, key_ids):
        key_rows = pair[:, 0].reshape(block_rows, local_heads, HD)
        value_rows = pair[:, 1].reshape(block_rows, local_heads, HD)

        def visit_one_span(span_items):
            return fold_block(
                (span_items[0], span_items[1], span_items[2]),
                span_items[3],
                span_items[4],
                key_rows,
                value_rows,
                key_ids,
                score_scale,
            )

        return lax.map(
            visit_one_span,
            (softmax_state[0], softmax_state[1], softmax_state[2], query_blocks, id_blocks),
        )

    softmax_state = (
        jnp.full((span_count, local_heads, span_rows), NEGATIVE, jnp.float32),
        jnp.zeros((span_count, local_heads, span_rows), jnp.float32),
        jnp.zeros((span_count, span_rows, local_heads, HD), jnp.float32),
    )
    softmax_state = visit_block(softmax_state, own_pair, query_ids)
    kept_below = None
    kept_above = None

    def forward_step(cycle_step, loop_carry):
        current_state, key_lower, key_upper, store_below, store_above = loop_carry
        key_lower = from_behind(key_lower, "blk", 1)
        key_upper = from_behind(key_upper, "blk", -1)
        low_ids = source_ids(position - cycle_step)
        high_ids = source_ids(position + cycle_step)
        current_state = lax.cond(
            meets(low_ids),
            lambda current: visit_block(current, key_lower, low_ids),
            lambda current: current,
            current_state,
        )
        current_state = lax.cond(
            meets(high_ids),
            lambda current: visit_block(current, key_upper, high_ids),
            lambda current: current,
            current_state,
        )
        return (current_state, key_lower, key_upper, store_below, store_above)

    softmax_state, spent_low, spent_high, kept_below, kept_above = lax.fori_loop(
        1, REACH + 1, forward_step, (softmax_state, own_pair, own_pair, kept_below, kept_above)
    )
    running, denominator, weighted = softmax_state
    context_full = weighted / jnp.transpose(denominator, (0, 2, 1))[:, :, :, None]
    log_sums = running + jnp.log(denominator)
    context_full = context_full.reshape(block_rows, local_heads, HD)
    context_low = context_full.astype(jnp.bfloat16).reshape(block_rows, 1, slab_width)
    context_tok = lax.all_to_all(
        context_low, "head", split_axis=0, concat_axis=1, tiled=True
    ).reshape(tok_rows, model_width)
    tokens_wide = tokens.astype(jnp.float32)
    attn_out = jnp.dot(context_tok, full_out, preferred_element_type=jnp.float32) + biases_all[2]
    mid_sum = tokens_wide + attn_out
    hidden, norm_first_back = jax.vjp(norm_rows, mid_sum, gains_all[0], shifts_all[0])
    hidden_low = hidden.astype(jnp.bfloat16)
    pre_act = jnp.dot(hidden_low, full_ff1, preferred_element_type=jnp.float32) + ff_shift
    activated, gelu_back = jax.vjp(gelu_exact, pre_act)
    act_low = activated.astype(jnp.bfloat16)
    ff_out = jnp.dot(act_low, full_ff2, preferred_element_type=jnp.float32) + biases_all[3]
    out_sum = hidden + ff_out
    result, norm_second_back = jax.vjp(norm_rows, out_sum, gains_all[1], shifts_all[1])
    out = result.astype(jnp.bfloat16)
    d_sum, gain_second, shift_second = norm_second_back(d_out.astype(jnp.float32))
    d_ff = d_sum.astype(jnp.bfloat16)
    grad_wff2 = jnp.einsum("tf,td->fd", act_low, d_ff, preferred_element_type=jnp.float32)
    bias_ff2 = jnp.sum(d_ff, axis=0, dtype=jnp.float32)
    d_act = jnp.einsum("td,fd->tf", d_ff, full_ff2, preferred_element_type=jnp.float32)
    d_pre = gelu_back(d_act)[0].astype(jnp.bfloat16)
    grad_wff1 = jnp.einsum("td,tf->df", hidden_low, d_pre, preferred_element_type=jnp.float32)
    grad_ffb = jnp.sum(d_pre, axis=0, dtype=jnp.float32)
    d_hidden = d_sum + jnp.einsum("tf,df->td", d_pre, full_ff1, preferred_element_type=jnp.float32)
    d_mid, gain_first, shift_first = norm_first_back(d_hidden)
    d_attn = d_mid.astype(jnp.bfloat16)
    grad_wout = jnp.einsum("tc,td->cd", context_tok, d_attn, preferred_element_type=jnp.float32)
    bias_out = jnp.sum(d_attn, axis=0, dtype=jnp.float32)
    d_context = jnp.einsum(
        "td,cd->tc", d_attn, full_out, preferred_element_type=jnp.float32
    ).astype(jnp.bfloat16)
    grad_heads = lax.all_to_all(
        d_context.reshape(tok_rows, groups, slab_width),
        "head",
        split_axis=1,
        concat_axis=0,
        tiled=True,
    ).reshape(block_rows, local_heads, HD)
    deltas = jnp.sum(grad_heads.astype(jnp.float32) * context_full, axis=2)
    delta_blocks = jnp.transpose(deltas.reshape(span_count, span_rows, local_heads), (0, 2, 1))
    grad_blocks = grad_heads.reshape(span_count, span_rows, local_heads, HD)
    own_set = (query_blocks, grad_blocks, log_sums, delta_blocks)

    def back_visit(pair, key_ids, query_set, query_id_blocks):
        key_rows = pair[:, 0].reshape(block_rows, local_heads, HD)
        value_rows = pair[:, 1].reshape(block_rows, local_heads, HD)

        def back_one_span(totals, span_items):
            grad_queries, grad_keys, grad_values = back_block(
                span_items[0],
                span_items[1],
                span_items[2],
                span_items[3],
                span_items[4],
                key_rows,
                value_rows,
                key_ids,
                score_scale,
            )
            totals = (totals[0] + grad_keys, totals[1] + grad_values)
            return (totals, grad_queries)

        zero_rows = jnp.zeros((block_rows, local_heads, HD), jnp.float32)
        start_totals = (zero_rows, zero_rows)
        totals, grad_queries = lax.scan(
            back_one_span,
            start_totals,
            (query_set[0], query_set[1], query_set[2], query_set[3], query_id_blocks),
        )
        query_part = grad_queries.reshape(block_rows, local_heads, HD)
        pair_part = None
        pair_part = jnp.stack([totals[0], totals[1]], axis=1).reshape(block_rows, 2, slab_width)
        return (query_part, pair_part)

    query_grad, own_grad = back_visit(own_pair, query_ids, own_set, id_blocks)
    zero_pair = jnp.zeros((block_rows, 2, slab_width), jnp.float32)

    def next_keys(key_lower, key_upper):
        key_lower = from_behind(key_lower, "blk", 1)
        key_upper = from_behind(key_upper, "blk", -1)
        return (key_lower, key_upper)

    def backward_step(cycle_step, loop_carry):
        query_acc, key_lower, key_upper, grad_low, grad_high = loop_carry
        key_lower, key_upper = next_keys(key_lower, key_upper)
        grad_low = from_behind(grad_low.astype(jnp.bfloat16), "blk", 1).astype(grad_low.dtype)
        grad_high = from_behind(grad_high.astype(jnp.bfloat16), "blk", -1).astype(grad_high.dtype)
        low_ids = source_ids(position - cycle_step)
        high_ids = source_ids(position + cycle_step)

        def add_low(current):
            found_query, found_pair = back_visit(key_lower, low_ids, own_set, id_blocks)
            return (current[0] + found_query, current[1] + found_pair)

        def add_high(current):
            found_query, found_pair = back_visit(key_upper, high_ids, own_set, id_blocks)
            return (current[0] + found_query, current[1] + found_pair)

        query_acc, grad_low = lax.cond(
            meets(low_ids), add_low, lambda current: current, (query_acc, grad_low)
        )
        query_acc, grad_high = lax.cond(
            meets(high_ids), add_high, lambda current: current, (query_acc, grad_high)
        )
        return (query_acc, key_lower, key_upper, grad_low, grad_high)

    query_grad, spent_low, spent_high, grad_low, grad_high = lax.fori_loop(
        1, REACH + 1, backward_step, (query_grad, own_pair, own_pair, zero_pair, zero_pair)
    )
    home_low = from_behind(grad_low.astype(jnp.bfloat16), "blk", -REACH).astype(grad_low.dtype)
    home_high = from_behind(grad_high.astype(jnp.bfloat16), "blk", REACH).astype(grad_high.dtype)
    pair_total = own_grad + home_low + home_high
    grad_stack = jnp.concatenate(
        [query_grad.reshape(block_rows, 1, slab_width), pair_total], axis=1
    )
    grad_stack = grad_stack.astype(jnp.bfloat16).reshape(block_rows, 3, 1, slab_width)
    grad_joined = lax.all_to_all(
        grad_stack, "head", split_axis=0, concat_axis=2, tiled=True
    ).reshape(tok_rows, 3 * model_width)
    grad_wqkv = jnp.einsum("td,tc->dc", tokens, grad_joined, preferred_element_type=jnp.float32)
    bias_query = jnp.sum(grad_joined[:, :model_width], axis=0, dtype=jnp.float32)
    bias_value = jnp.sum(grad_joined[:, 2 * model_width :], axis=0, dtype=jnp.float32)
    d_tokens = (
        d_mid + jnp.einsum("tc,dc->td", grad_joined, full_qkv, preferred_element_type=jnp.float32)
    ).astype(jnp.bfloat16)
    grad_terms = (
        grad_wqkv,
        grad_wout,
        grad_wff1,
        grad_wff2,
        jnp.stack([gain_first, gain_second]),
        jnp.stack([shift_first, shift_second]),
        jnp.stack([bias_query, bias_value, bias_out, bias_ff2]),
        grad_ffb,
    )
    owned_grads = (
        lax.psum_scatter(grad_terms[0], ("blk", "head"), scatter_dimension=0, tiled=True),
        lax.psum_scatter(grad_terms[1], ("blk", "head"), scatter_dimension=0, tiled=True),
        lax.psum_scatter(grad_terms[2], ("blk", "head"), scatter_dimension=0, tiled=True),
        lax.psum_scatter(grad_terms[3], ("blk", "head"), scatter_dimension=0, tiled=True),
        lax.psum_scatter(grad_terms[4], ("blk", "head"), scatter_dimension=1, tiled=True),
        lax.psum_scatter(grad_terms[5], ("blk", "head"), scatter_dimension=1, tiled=True),
        lax.psum_scatter(grad_terms[6], ("blk", "head"), scatter_dimension=1, tiled=True),
        lax.psum_scatter(grad_terms[7], ("blk", "head"), scatter_dimension=0, tiled=True),
    )
    return (
        out,
        d_tokens,
        owned_grads[0],
        owned_grads[1],
        owned_grads[2],
        owned_grads[3],
        owned_grads[4],
        owned_grads[5],
        owned_grads[6],
        owned_grads[7],
    )


def solution(mesh):
    in_specs = (
        P(("blk", "head"), None),
        P(("blk", "head"), None),
        P(("blk", "head"), None),
        P(("blk", "head"), None),
        P(("blk", "head"), None),
        P(None, ("blk", "head")),
        P(None, ("blk", "head")),
        P(None, ("blk", "head")),
        P(("blk", "head")),
        P(),
        P(("blk", "head"), None),
    )
    out_specs = (
        P(("blk", "head"), None),
        P(("blk", "head"), None),
        P(("blk", "head"), None),
        P(("blk", "head"), None),
        P(("blk", "head"), None),
        P(("blk", "head"), None),
        P(None, ("blk", "head")),
        P(None, ("blk", "head")),
        P(None, ("blk", "head")),
        P(("blk", "head")),
    )
    return jax.shard_map(body, mesh=mesh, in_specs=in_specs, out_specs=out_specs, check_vma=False)
```

profile of v0, /device:TPU:0, one launch (start us, length us, event | category | flops | bytes accessed | tf_op | source)
XLA Modules:
  0.0 1146.2 jit_solution(4280274502822187792)
XLA Ops:
  13.3 70.1 %all-gather = bf16[32,24,4]{1,2,0:T(4,128)(2,1)S(1)} all-gather(bf16[1,24,4]{1,2,0:T(4,128)(2,1)} %bitcast.324), channel_id=1, replica_groups=mesh['head'=2,'blk'=16] {'blk','head'}, dimensions={0}, use_global_device_ids=true | all-gather | bytes 6336 | tf_op jit(solution)/shard_map/all_gather | solution.py:113
  92.4 69.3 %all-gather.1 = bf16[32,24,2]{1,2,0:T(2,128)(2,1)S(1)} all-gather(bf16[1,24,2]{1,2,0:T(2,128)(2,1)S(1)} %bitcast.325), channel_id=1, replica_groups=mesh['head'=2,'blk'=16] {'blk','head'}, dimensions={0}, use_global_device_ids=true | all-gather | bytes 3168 | tf_op jit(solution)/shard_map/all_gather | solution.py:111
  161.9 64.7 %all-gather.2 = bf16[32,24,2]{1,2,0:T(2,128)(2,1)S(1)} all-gather(bf16[1,24,2]{1,2,0:T(2,128)(2,1)S(1)} %bitcast.326), channel_id=1, replica_groups=mesh['head'=2,'blk'=16] {'blk','head'}, dimensions={0}, use_global_device_ids=true | all-gather | bytes 3168 | tf_op jit(solution)/shard_map/all_gather | solution.py:112
  228.4 37.8 %all-reduce = bf16[3072]{0:T(1024)(128)(2,1)S(1)} all-reduce(bf16[3072]{0:T(1024)(128)(2,1)S(1)} %dynamic-update-slice), channel_id=1, replica_groups=mesh['head'=2,'blk'=16] {'blk','head'}, use_global_device_ids=true, to_apply=%add | all-reduce | flops 3072 | bytes 12288
  275.6 106.3 %while.40 = (s32[]{:T(128)}, f32[1,6,512]{2,1,0:T(8,128)S(1)}, f32[1,6,512]{2,1,0:T(8,128)S(1)}, f32[1,512,6,64]{1,3,2,0:T(8,128)}, bf16[512,2,384]{0,2,1:T(8,12...) while((s32[]{:T(128)}, f32[1,6,512]{2,1,0:T(8,128)S(1)}, ...), condition=%wide.region_18.19_spmd, body=%wide.region_4.18_spmd.sunk | while | flops 842404992 | bytes 58349588 | solution.py:204
  290.5 6.7 conditional.8
  297.2 6.7 conditional.9
  319.4 6.7 conditional.8
  327.1 18.0 %collective-permute-start = (bf16[512,2,384]{0,2,1:T(8,128)(2,1)}, bf16[512,2,384]{0,2,1:T(8,128)(2,1)S(1)}, u32[]{:S(2)}, u32[]{:S(2)}) collective-permute-start(bf16[512,2,384]{0,2,1:T(8,128)(2,1)} %get-tuple-element.1738), channel_id=1, source_target_pairs={{0,1},{1,2},{2,3},{3,4},{4,5},{5,6},{6,7},{7,8},{8,9},{9,10},{10,1... | collective-permute-start | bytes 2359304 | tf_op jit(solution)/shard_map/while/body/eval_jaxpr/ppermute | solution.py:18
  351.0 6.7 conditional.8
  358.8 12.7 %collective-permute-start = (bf16[512,2,384]{0,2,1:T(8,128)(2,1)}, bf16[512,2,384]{0,2,1:T(8,128)(2,1)S(1)}, u32[]{:S(2)}, u32[]{:S(2)}) collective-permute-start(bf16[512,2,384]{0,2,1:T(8,128)(2,1)} %get-tuple-element.1738), channel_id=1, source_target_pairs={{0,1},{1,2},{2,3},{3,4},{4,5},{5,6},{6,7},{7,8},{8,9},{9,10},{10,1... | collective-permute-start | bytes 2359304 | tf_op jit(solution)/shard_map/while/body/eval_jaxpr/ppermute | solution.py:18
  439.3 214.7 %while.41 = (s32[]{:T(128)}, f32[512,6,64]{0,2,1:T(8,128)}, bf16[512,2,384]{0,2,1:T(8,128)(2,1)}, bf16[512,2,384]{0,2,1:T(8,128)(2,1)}, f32[512,2,384]{0,2,1:T(8...) while((s32[]{:T(128)}, f32[512,6,64]{0,2,1:T(8,128)}, ...), condition=%wide.region_38.39_spmd, body=%wide.region_28.38_spmd.sunk | while | flops 2057027712 | bytes 123796416 | solution.py:318
  440.7 12.6 %collective-permute-start.2 = (bf16[512,2,384]{0,2,1:T(8,128)(2,1)}, bf16[512,2,384]{0,2,1:T(8,128)(2,1)}, u32[]{:S(2)}, u32[]{:S(2)}) collective-permute-start(bf16[512,2,384]{0,2,1:T(8,128)(2,1)} %convert_element_type.434), channel_id=1, source_target_pairs={{0,1},{1,2},{2,3},{3,4},{4,5},{5,6},{6,7},{7,8},{8,9},{9,10},{10,1... | collective-permute-start | bytes 2359304 | tf_op jit(solution)/shard_map/while/body/eval_jaxpr/ppermute | solution.py:18
  468.4 11.6 %conditional.10 = ((f32[512,6,64]{0,2,1:T(8,128)}, f32[512,2,384]{0,2,1:T(8,128)S(1)})) conditional(s32[]{:T(128)} %convert_element_type.433, (f32[512,6,64]{0,2,1:T(8,128)}, f32[512,2,384]{0,2,1:T(8,128)S(1)}) %tuple.220, (s32[1,512]{1,0:T(1,128)S(1)}, s32[512]{0:T(512)S(1)}, pred[512]{0:T(512)(128)(4,1)}, s32[512]{0:T(512)S(1)}, ...), branch_computations={%region_34.34_spmd, %region_35.35_spmd} | conditional | flops 1027148800 | bytes 49298084 | solution.py:310
  481.4 11.6 %conditional.11 = ((f32[512,6,64]{0,2,1:T(8,128)}, f32[512,2,384]{0,2,1:T(8,128)S(1)})) conditional(s32[]{:T(128)} %convert_element_type.432, (f32[512,6,64]{0,2,1:T(8,128)}, f32[512,2,384]{0,2,1:T(8,128)S(1)}) %tuple.222, (s32[1,512]{1,0:T(1,128)S(1)}, s32[512]{0:T(512)S(1)}, pred[512]{0:T(512)(128)(4,1)}, s32[512]{0:T(512)S(1)}, ...), branch_computations={%region_36.36_spmd, %region_37.37_spmd} | conditional | flops 1027148800 | bytes 49298084 | solution.py:313
  498.2 12.8 %collective-permute-start.2 = (bf16[512,2,384]{0,2,1:T(8,128)(2,1)}, bf16[512,2,384]{0,2,1:T(8,128)(2,1)}, u32[]{:S(2)}, u32[]{:S(2)}) collective-permute-start(bf16[512,2,384]{0,2,1:T(8,128)(2,1)} %convert_element_type.434), channel_id=1, source_target_pairs={{0,1},{1,2},{2,3},{3,4},{4,5},{5,6},{6,7},{7,8},{8,9},{9,10},{10,1... | collective-permute-start | bytes 2359304 | tf_op jit(solution)/shard_map/while/body/eval_jaxpr/ppermute | solution.py:18
  516.5 7.5 collective-permute-start.5
  531.7 11.6 %conditional.10 = ((f32[512,6,64]{0,2,1:T(8,128)}, f32[512,2,384]{0,2,1:T(8,128)S(1)})) conditional(s32[]{:T(128)} %convert_element_type.433, (f32[512,6,64]{0,2,1:T(8,128)}, f32[512,2,384]{0,2,1:T(8,128)S(1)}) %tuple.220, (s32[1,512]{1,0:T(1,128)S(1)}, s32[512]{0:T(512)S(1)}, pred[512]{0:T(512)(128)(4,1)}, s32[512]{0:T(512)S(1)}, ...), branch_computations={%region_34.34_spmd, %region_35.35_spmd} | conditional | flops 1027148800 | bytes 49298084 | solution.py:310
  549.9 24.3 %collective-permute-start.2 = (bf16[512,2,384]{0,2,1:T(8,128)(2,1)}, bf16[512,2,384]{0,2,1:T(8,128)(2,1)}, u32[]{:S(2)}, u32[]{:S(2)}) collective-permute-start(bf16[512,2,384]{0,2,1:T(8,128)(2,1)} %convert_element_type.434), channel_id=1, source_target_pairs={{0,1},{1,2},{2,3},{3,4},{4,5},{5,6},{6,7},{7,8},{8,9},{9,10},{10,1... | collective-permute-start | bytes 2359304 | tf_op jit(solution)/shard_map/while/body/eval_jaxpr/ppermute | solution.py:18
  589.3 11.6 %conditional.10 = ((f32[512,6,64]{0,2,1:T(8,128)}, f32[512,2,384]{0,2,1:T(8,128)S(1)})) conditional(s32[]{:T(128)} %convert_element_type.433, (f32[512,6,64]{0,2,1:T(8,128)}, f32[512,2,384]{0,2,1:T(8,128)S(1)}) %tuple.220, (s32[1,512]{1,0:T(1,128)S(1)}, s32[512]{0:T(512)S(1)}, pred[512]{0:T(512)(128)(4,1)}, s32[512]{0:T(512)S(1)}, ...), branch_computations={%region_34.34_spmd, %region_35.35_spmd} | conditional | flops 1027148800 | bytes 49298084 | solution.py:310
  607.5 16.6 %collective-permute-start.2 = (bf16[512,2,384]{0,2,1:T(8,128)(2,1)}, bf16[512,2,384]{0,2,1:T(8,128)(2,1)}, u32[]{:S(2)}, u32[]{:S(2)}) collective-permute-start(bf16[512,2,384]{0,2,1:T(8,128)(2,1)} %convert_element_type.434), channel_id=1, source_target_pairs={{0,1},{1,2},{2,3},{3,4},{4,5},{5,6},{6,7},{7,8},{8,9},{9,10},{10,1... | collective-permute-start | bytes 2359304 | tf_op jit(solution)/shard_map/while/body/eval_jaxpr/ppermute | solution.py:18
  629.6 10.2 collective-permute-start.5
  656.0 9.1 collective-permute-start.6
  677.7 6.1 collective-permute-done.7
  688.7 14.8 %all_to_all.63 = bf16[512,3,1,384]{3,1,2,0:T(4,128)(2,1)S(1)} all-to-all(bf16[512,3,1,384]{3,1,2,0:T(4,128)(2,1)S(1)} %pad_maximum_fusion), channel_id=1, replica_groups=mesh['head'=2,'blk'=16] {'head'}, dimensions={0} | all-to-all | bytes 2359296 | tf_op jit(solution)/shard_map/all_to_all | solution.py:328
  708.3 8.0 copy.309
  717.5 6.6 fusion.115
  725.1 6.5 fusion.129
  733.6 59.5 %all-reduce.5 = (f32[2,768]{1,0:T(2,128)S(1)}, f32[2,768]{1,0:T(2,128)S(1)}, f32[4,768]{1,0:T(4,128)S(1)}, f32[3072]{0:T(1024)S(1)}) all-reduce(f32[2,768]{1,0:T(2,128)S(1)} %pad_maximum_fusion.3, f32[2,768]{1,0:T(2,128)S(1)} %pad_maximum_fusion.4, ...), channel_id=6, replica_groups=mesh['head'=2,'blk'=16] {'blk','head'}, use_global_device_ids=true, to_apply=%region_45.46.clone | all-reduce | flops 9216 | bytes 73728
  799.5 56.4 %reduce-scatter.16.cloned.1.call-done = f32[24,2304]{1,0:T(8,128)} async-done(((f32[768,2304]{1,0:T(8,128)}), f32[24,2304]{1,0:T(8,128)}) %reduce-scatter.16.cloned.1.call-update) | async-done | bytes 221200
  855.9 141.2 %reduce-scatter.12.cloned.1.call-done = f32[24,3072]{1,0:T(8,128)} async-done(((f32[768,3072]{1,0:T(8,128)}), f32[24,3072]{1,0:T(8,128)}) %reduce-scatter.12.cloned.1.call-update) | async-done | bytes 294928 | tf_op jit(solution)/shard_map/reduce_scatter | solution.py:350
  997.1 142.1 %reduce-scatter.14.cloned.1.call-done = f32[96,768]{1,0:T(8,128)} async-done(((f32[3072,768]{1,0:T(8,128)}), f32[96,768]{1,0:T(8,128)}) %reduce-scatter.14.cloned.1.call-update) | async-done | bytes 294928 | tf_op jit(solution)/shard_map/reduce_scatter | solution.py:351
  (491 shorter events, 297.8 us)
Async XLA Ops:
  7.2 76.6 %all-gather.8.cloned.1.call-start = ((), (), s32[]{:S(2)}) async-start(), calls=%async_computation.8 | async-start | bytes 3649536 | tf_op jit(solution)/shard_map/all_gather | solution.py:107
  7.9 388.0 %all-gather.10.cloned.1.call-start = ((), (), s32[]{:S(2)}) async-start(), calls=%async_computation.9 | async-start | bytes 1216512 | tf_op jit(solution)/shard_map/all_gather | solution.py:108
  8.7 389.4 %all-gather.12.cloned.1.call-start = ((), (), s32[]{:S(2)}) async-start(), calls=%async_computation.10 | async-start | bytes 4866048 | tf_op jit(solution)/shard_map/all_gather | solution.py:109
  9.4 394.7 %all-gather.14.cloned.1.call-start = ((), (), s32[]{:S(2)}) async-start(), calls=%async_computation.11 | async-start | bytes 4866048 | tf_op jit(solution)/shard_map/all_gather | solution.py:110
  88.6 178.6 %all-to-all-start = ((bf16[256,3,2,384]{3,0,1,2:T(8,128)(2,1)}), bf16[256,3,2,384]{3,0,1,2:T(8,128)(2,1)S(1)}, u32[]{:S(2)}, u32[]{:S(2)}) async-start(bf16[256,3,2,384]{3,0,1,2:T(8,128)(2,1)} %copy.270), calls=%async_computation | async-start | bytes 2359296 | tf_op jit(solution)/shard_map/all_to_all | solution.py:140
  276.0 14.5 %collective-permute-start = (bf16[512,2,384]{0,2,1:T(8,128)(2,1)}, bf16[512,2,384]{0,2,1:T(8,128)(2,1)S(1)}, u32[]{:S(2)}, u32[]{:S(2)}) collective-permute-start(bf16[512,2,384]{0,2,1:T(8,128)(2,1)} %get-tuple-element.1738), channel_id=1, source_target_pairs={{0,1},{1,2},{2,3},{3,4},{4,5},{5,6},{6,7},{7,8},{8,9},{9,10},{10,1... | collective-permute-start | bytes 2359304 | tf_op jit(solution)/shard_map/while/body/eval_jaxpr/ppermute | solution.py:18
  276.1 21.1 %collective-permute-start.1 = (bf16[512,2,384]{0,2,1:T(8,128)(2,1)S(1)}, bf16[512,2,384]{0,2,1:T(8,128)(2,1)S(1)}, u32[]{:S(2)}, u32[]{:S(2)}) collective-permute-start(bf16[512,2,384]{0,2,1:T(8,128)(2,1)S(1)} %get-tuple-element.1739), channel_id=1, source_target_pairs={{0,15},{1,0},{2,1},{3,2},{4,3},{5,4},{6,5},{7,6},{8,7},{9,8},{10,9... | collective-permute-start | bytes 2359304 | tf_op jit(solution)/shard_map/while/body/eval_jaxpr/ppermute | solution.py:18
  310.6 15.5 %collective-permute-start.1 = (bf16[512,2,384]{0,2,1:T(8,128)(2,1)S(1)}, bf16[512,2,384]{0,2,1:T(8,128)(2,1)S(1)}, u32[]{:S(2)}, u32[]{:S(2)}) collective-permute-start(bf16[512,2,384]{0,2,1:T(8,128)(2,1)S(1)} %get-tuple-element.1739), channel_id=1, source_target_pairs={{0,15},{1,0},{2,1},{3,2},{4,3},{5,4},{6,5},{7,6},{8,7},{9,8},{10,9... | collective-permute-start | bytes 2359304 | tf_op jit(solution)/shard_map/while/body/eval_jaxpr/ppermute | solution.py:18
  327.1 23.9 %collective-permute-start = (bf16[512,2,384]{0,2,1:T(8,128)(2,1)}, bf16[512,2,384]{0,2,1:T(8,128)(2,1)S(1)}, u32[]{:S(2)}, u32[]{:S(2)}) collective-permute-start(bf16[512,2,384]{0,2,1:T(8,128)(2,1)} %get-tuple-element.1738), channel_id=1, source_target_pairs={{0,1},{1,2},{2,3},{3,4},{4,5},{5,6},{6,7},{7,8},{8,9},{9,10},{10,1... | collective-permute-start | bytes 2359304 | tf_op jit(solution)/shard_map/while/body/eval_jaxpr/ppermute | solution.py:18
  358.8 18.6 %collective-permute-start = (bf16[512,2,384]{0,2,1:T(8,128)(2,1)}, bf16[512,2,384]{0,2,1:T(8,128)(2,1)S(1)}, u32[]{:S(2)}, u32[]{:S(2)}) collective-permute-start(bf16[512,2,384]{0,2,1:T(8,128)(2,1)} %get-tuple-element.1738), channel_id=1, source_target_pairs={{0,1},{1,2},{2,3},{3,4},{4,5},{5,6},{6,7},{7,8},{8,9},{9,10},{10,1... | collective-permute-start | bytes 2359304 | tf_op jit(solution)/shard_map/while/body/eval_jaxpr/ppermute | solution.py:18
  423.4 376.1 %reduce-scatter.10.cloned.1.call-start = ((), (), s32[]{:S(2)}) async-start(), calls=%async_computation.12 | async-start | bytes 2433024 | tf_op jit(solution)/shard_map/reduce_scatter | solution.py:349
  425.4 430.5 %reduce-scatter.16.cloned.1.call-start = ((), (), s32[]{:S(2)}) async-start(), calls=%async_computation.15 | async-start | bytes 7299072
  440.7 23.9 %collective-permute-start.2 = (bf16[512,2,384]{0,2,1:T(8,128)(2,1)}, bf16[512,2,384]{0,2,1:T(8,128)(2,1)}, u32[]{:S(2)}, u32[]{:S(2)}) collective-permute-start(bf16[512,2,384]{0,2,1:T(8,128)(2,1)} %convert_element_type.434), channel_id=1, source_target_pairs={{0,1},{1,2},{2,3},{3,4},{4,5},{5,6},{6,7},{7,8},{8,9},{9,10},{10,1... | collective-permute-start | bytes 2359304 | tf_op jit(solution)/shard_map/while/body/eval_jaxpr/ppermute | solution.py:18
  453.3 14.5 %collective-permute-start.3 = (bf16[512,2,384]{0,2,1:T(8,128)(2,1)}, bf16[512,2,384]{0,2,1:T(8,128)(2,1)}, u32[]{:S(2)}, u32[]{:S(2)}) collective-permute-start(bf16[512,2,384]{0,2,1:T(8,128)(2,1)} %get-tuple-element.1787), channel_id=1, source_target_pairs={{0,1},{1,2},{2,3},{3,4},{4,5},{5,6},{6,7},{7,8},{8,9},{9,10},{10,1... | collective-permute-start | bytes 2359304 | tf_op jit(solution)/shard_map/while/body/eval_jaxpr/ppermute | solution.py:18
  454.3 25.7 %collective-permute-start.4 = (bf16[512,2,384]{0,2,1:T(8,128)(2,1)}, bf16[512,2,384]{0,2,1:T(8,128)(2,1)}, u32[]{:S(2)}, u32[]{:S(2)}) collective-permute-start(bf16[512,2,384]{0,2,1:T(8,128)(2,1)} %convert_element_type.436), channel_id=1, source_target_pairs={{0,15},{1,0},{2,1},{3,2},{4,3},{5,4},{6,5},{7,6},{8,7},{9,8},{10,9... | collective-permute-start | bytes 2359304 | tf_op jit(solution)/shard_map/while/body/eval_jaxpr/ppermute | solution.py:18
  458.8 22.6 %collective-permute-start.5 = (bf16[512,2,384]{0,2,1:T(8,128)(2,1)}, bf16[512,2,384]{0,2,1:T(8,128)(2,1)}, u32[]{:S(2)}, u32[]{:S(2)}) collective-permute-start(bf16[512,2,384]{0,2,1:T(8,128)(2,1)} %get-tuple-element.1788), channel_id=1, source_target_pairs={{0,15},{1,0},{2,1},{3,2},{4,3},{5,4},{6,5},{7,6},{8,7},{9,8},{10,9... | collective-permute-start | bytes 2359304 | tf_op jit(solution)/shard_map/while/body/eval_jaxpr/ppermute | solution.py:18
  498.2 31.6 %collective-permute-start.2 = (bf16[512,2,384]{0,2,1:T(8,128)(2,1)}, bf16[512,2,384]{0,2,1:T(8,128)(2,1)}, u32[]{:S(2)}, u32[]{:S(2)}) collective-permute-start(bf16[512,2,384]{0,2,1:T(8,128)(2,1)} %convert_element_type.434), channel_id=1, source_target_pairs={{0,1},{1,2},{2,3},{3,4},{4,5},{5,6},{6,7},{7,8},{8,9},{9,10},{10,1... | collective-permute-start | bytes 2359304 | tf_op jit(solution)/shard_map/while/body/eval_jaxpr/ppermute | solution.py:18
  511.0 20.1 %collective-permute-start.3 = (bf16[512,2,384]{0,2,1:T(8,128)(2,1)}, bf16[512,2,384]{0,2,1:T(8,128)(2,1)}, u32[]{:S(2)}, u32[]{:S(2)}) collective-permute-start(bf16[512,2,384]{0,2,1:T(8,128)(2,1)} %get-tuple-element.1787), channel_id=1, source_target_pairs={{0,1},{1,2},{2,3},{3,4},{4,5},{5,6},{6,7},{7,8},{8,9},{9,10},{10,1... | collective-permute-start | bytes 2359304 | tf_op jit(solution)/shard_map/while/body/eval_jaxpr/ppermute | solution.py:18
  514.5 28.8 %collective-permute-start.4 = (bf16[512,2,384]{0,2,1:T(8,128)(2,1)}, bf16[512,2,384]{0,2,1:T(8,128)(2,1)}, u32[]{:S(2)}, u32[]{:S(2)}) collective-permute-start(bf16[512,2,384]{0,2,1:T(8,128)(2,1)} %convert_element_type.436), channel_id=1, source_target_pairs={{0,15},{1,0},{2,1},{3,2},{4,3},{5,4},{6,5},{7,6},{8,7},{9,8},{10,9... | collective-permute-start | bytes 2359304 | tf_op jit(solution)/shard_map/while/body/eval_jaxpr/ppermute | solution.py:18
  516.5 28.2 %collective-permute-start.5 = (bf16[512,2,384]{0,2,1:T(8,128)(2,1)}, bf16[512,2,384]{0,2,1:T(8,128)(2,1)}, u32[]{:S(2)}, u32[]{:S(2)}) collective-permute-start(bf16[512,2,384]{0,2,1:T(8,128)(2,1)} %get-tuple-element.1788), channel_id=1, source_target_pairs={{0,15},{1,0},{2,1},{3,2},{4,3},{5,4},{6,5},{7,6},{8,7},{9,8},{10,9... | collective-permute-start | bytes 2359304 | tf_op jit(solution)/shard_map/while/body/eval_jaxpr/ppermute | solution.py:18
  549.9 35.6 %collective-permute-start.2 = (bf16[512,2,384]{0,2,1:T(8,128)(2,1)}, bf16[512,2,384]{0,2,1:T(8,128)(2,1)}, u32[]{:S(2)}, u32[]{:S(2)}) collective-permute-start(bf16[512,2,384]{0,2,1:T(8,128)(2,1)} %convert_element_type.434), channel_id=1, source_target_pairs={{0,1},{1,2},{2,3},{3,4},{4,5},{5,6},{6,7},{7,8},{8,9},{9,10},{10,1... | collective-permute-start | bytes 2359304 | tf_op jit(solution)/shard_map/while/body/eval_jaxpr/ppermute | solution.py:18
  574.2 14.5 %collective-permute-start.3 = (bf16[512,2,384]{0,2,1:T(8,128)(2,1)}, bf16[512,2,384]{0,2,1:T(8,128)(2,1)}, u32[]{:S(2)}, u32[]{:S(2)}) collective-permute-start(bf16[512,2,384]{0,2,1:T(8,128)(2,1)} %get-tuple-element.1787), channel_id=1, source_target_pairs={{0,1},{1,2},{2,3},{3,4},{4,5},{5,6},{6,7},{7,8},{8,9},{9,10},{10,1... | collective-permute-start | bytes 2359304 | tf_op jit(solution)/shard_map/while/body/eval_jaxpr/ppermute | solution.py:18
  575.2 25.7 %collective-permute-start.4 = (bf16[512,2,384]{0,2,1:T(8,128)(2,1)}, bf16[512,2,384]{0,2,1:T(8,128)(2,1)}, u32[]{:S(2)}, u32[]{:S(2)}) collective-permute-start(bf16[512,2,384]{0,2,1:T(8,128)(2,1)} %convert_element_type.436), channel_id=1, source_target_pairs={{0,15},{1,0},{2,1},{3,2},{4,3},{5,4},{6,5},{7,6},{8,7},{9,8},{10,9... | collective-permute-start | bytes 2359304 | tf_op jit(solution)/shard_map/while/body/eval_jaxpr/ppermute | solution.py:18
  579.7 22.6 %collective-permute-start.5 = (bf16[512,2,384]{0,2,1:T(8,128)(2,1)}, bf16[512,2,384]{0,2,1:T(8,128)(2,1)}, u32[]{:S(2)}, u32[]{:S(2)}) collective-permute-start(bf16[512,2,384]{0,2,1:T(8,128)(2,1)} %get-tuple-element.1788), channel_id=1, source_target_pairs={{0,15},{1,0},{2,1},{3,2},{4,3},{5,4},{6,5},{7,6},{8,7},{9,8},{10,9... | collective-permute-start | bytes 2359304 | tf_op jit(solution)/shard_map/while/body/eval_jaxpr/ppermute | solution.py:18
  607.5 38.1 %collective-permute-start.2 = (bf16[512,2,384]{0,2,1:T(8,128)(2,1)}, bf16[512,2,384]{0,2,1:T(8,128)(2,1)}, u32[]{:S(2)}, u32[]{:S(2)}) collective-permute-start(bf16[512,2,384]{0,2,1:T(8,128)(2,1)} %convert_element_type.434), channel_id=1, source_target_pairs={{0,1},{1,2},{2,3},{3,4},{4,5},{5,6},{6,7},{7,8},{8,9},{9,10},{10,1... | collective-permute-start | bytes 2359304 | tf_op jit(solution)/shard_map/while/body/eval_jaxpr/ppermute | solution.py:18
  624.1 22.8 %collective-permute-start.3 = (bf16[512,2,384]{0,2,1:T(8,128)(2,1)}, bf16[512,2,384]{0,2,1:T(8,128)(2,1)}, u32[]{:S(2)}, u32[]{:S(2)}) collective-permute-start(bf16[512,2,384]{0,2,1:T(8,128)(2,1)} %get-tuple-element.1787), channel_id=1, source_target_pairs={{0,1},{1,2},{2,3},{3,4},{4,5},{5,6},{6,7},{7,8},{8,9},{9,10},{10,1... | collective-permute-start | bytes 2359304 | tf_op jit(solution)/shard_map/while/body/eval_jaxpr/ppermute | solution.py:18
  625.1 22.4 %collective-permute-start.4 = (bf16[512,2,384]{0,2,1:T(8,128)(2,1)}, bf16[512,2,384]{0,2,1:T(8,128)(2,1)}, u32[]{:S(2)}, u32[]{:S(2)}) collective-permute-start(bf16[512,2,384]{0,2,1:T(8,128)(2,1)} %convert_element_type.436), channel_id=1, source_target_pairs={{0,15},{1,0},{2,1},{3,2},{4,3},{5,4},{6,5},{7,6},{8,7},{9,8},{10,9... | collective-permute-start | bytes 2359304 | tf_op jit(solution)/shard_map/while/body/eval_jaxpr/ppermute | solution.py:18
  629.6 20.0 %collective-permute-start.5 = (bf16[512,2,384]{0,2,1:T(8,128)(2,1)}, bf16[512,2,384]{0,2,1:T(8,128)(2,1)}, u32[]{:S(2)}, u32[]{:S(2)}) collective-permute-start(bf16[512,2,384]{0,2,1:T(8,128)(2,1)} %get-tuple-element.1788), channel_id=1, source_target_pairs={{0,15},{1,0},{2,1},{3,2},{4,3},{5,4},{6,5},{7,6},{8,7},{9,8},{10,9... | collective-permute-start | bytes 2359304 | tf_op jit(solution)/shard_map/while/body/eval_jaxpr/ppermute | solution.py:18
  656.0 21.8 %collective-permute-start.6 = (bf16[512,2,384]{2,1,0:T(2,128)(2,1)}, bf16[512,2,384]{2,1,0:T(2,128)(2,1)}, u32[]{:S(2)}, u32[]{:S(2)}) collective-permute-start(bf16[512,2,384]{2,1,0:T(2,128)(2,1)} %copy.296), channel_id=1, source_target_pairs={{0,12},{1,13},{2,14},{3,15},{4,0},{5,1},{6,2},{7,3},{8,4},{9,5},{1... | collective-permute-start | bytes 2359304 | tf_op jit(solution)/shard_map/ppermute | solution.py:18
  667.1 16.7 %collective-permute-start.7 = (bf16[512,2,384]{2,1,0:T(2,128)(2,1)}, bf16[512,2,384]{2,1,0:T(2,128)(2,1)}, u32[]{:S(2)}, u32[]{:S(2)}) collective-permute-start(bf16[512,2,384]{2,1,0:T(2,128)(2,1)} %copy.297), channel_id=1, source_target_pairs={{0,4},{1,5},{2,6},{3,7},{4,8},{5,9},{6,10},{7,11},{8,12},{9,13},{1... | collective-permute-start | bytes 2359304 | tf_op jit(solution)/shard_map/ppermute | solution.py:18
  716.4 280.6 %reduce-scatter.12.cloned.1.call-start = ((), (), s32[]{:S(2)}) async-start(), calls=%async_computation.13 | async-start | bytes 9732096 | tf_op jit(solution)/shard_map/reduce_scatter | solution.py:350
  724.2 415.0 %reduce-scatter.14.cloned.1.call-start = ((), (), s32[]{:S(2)}) async-start(), calls=%async_computation.14 | async-start | bytes 9732096 | tf_op jit(solution)/shard_map/reduce_scatter | solution.py:351
  (75 other events, 1291.8 us)
Sparse Core Ops, SparseCore 0:
  10.9 63.0 all-gather.7
  76.9 53.0 all-gather.9
  132.9 62.5 all-gather.11
  198.3 63.0 all-gather.13
  429.8 127.5 reduce-scatter.9
  716.5 139.2 reduce-scatter.15
  862.3 134.6 reduce-scatter.11
  1004.5 134.5 reduce-scatter.13
where the time goes:
time: 1160 us; the launch traced here: 1150 us
  waiting for transfers between devices  373 us (32%)
  blocking collectives  316 us (27%)
  starting transfers between devices  163 us (14%)
  matrix products  112 us (10%)
  other arithmetic  74 us (6%)
  local copies, waits for them, and re-layouts  66.1 us (6%)
  loops' own time  22.6 us (2%)
  between operations  18.8 us (2%)
    ppermute x26, starting transfers between devices, from_behind(): return lax.ppermute(value, axis, pairs)  152 us
    reduce_scatter x1, waiting for transfers between devices, body(): lax.psum_scatter(grad_terms[3], ('blk', 'head'), scatter_dimension=0, til...  142 us
    reduce_scatter x1, waiting for transfers between devices, body(): lax.psum_scatter(grad_terms[2], ('blk', 'head'), scatter_dimension=0, til...  141 us
    unnamed x2, blocking collectives  97.3 us
    all_gather x1, blocking collectives, body(): lax.all_gather(proj_biases, ('blk', 'head'), axis=1, tiled=True)  70.1 us
    all_gather x1, blocking collectives, body(): lax.all_gather(norm_gains, ('blk', 'head'), axis=1, tiled=True)  69.3 us
    all_gather x1, blocking collectives, body(): lax.all_gather(norm_biases, ('blk', 'head'), axis=1, tiled=True)  64.7 us
    unnamed x9, waiting for transfers between devices  59 us
  transfers between devices with their start and end apart: 37, of which 12 were waited for; matrix products, arithmetic and copies ran while one was open for 20% of the time, Pallas kernels for 0%

commit v1 on v0

v1 whole, which is shorter than its diff:
```python
import functools

import jax
import jax.numpy as jnp
from jax import lax
from jax.experimental import pallas as pl
from jax.experimental.pallas import tpu as pltpu
from jax.sharding import PartitionSpec as P

H = 12
HD = 64
DOC_MOST = 2048
EPSILON = 1e-06
NEGATIVE = -1e30
MESH = pl.DeviceIdType.MESH
F32 = jnp.float32
BF16 = jnp.bfloat16
VMEM_BYTES = 60 * 1024 * 1024
CHIPS = 4
GROUP = 4
QW = 256
KW = 384
HW = (H // CHIPS) * HD


def div(a, b):
    return lax.div(a, jnp.int32(b))


def rem(a, b):
    return lax.rem(a, jnp.int32(b))


def nn(a, b):
    return lax.dot_general(a, b, (((1,), (0,)), ((), ())), preferred_element_type=F32)


def nt(a, b):
    return lax.dot_general(a, b, (((1,), (1,)), ((), ())), preferred_element_type=F32)


def tn(a, b):
    return lax.dot_general(a, b, (((0,), (0,)), ((), ())), preferred_element_type=F32)


def rows_at(start, count, unit=16):
    return pl.ds(pl.multiple_of(start, unit), count)


class Place:
    def __init__(self, repeat, groups):
        self.repeat = repeat
        blk, head = lax.axis_index("blk"), lax.axis_index("head")
        self.index = blk * 2 + head
        self.unit = div(self.index, repeat)
        self.core, self.x, self.y = rem(blk, 2), rem(div(blk, 2), 2), head
        self.group, self.groups = div(blk, GROUP), groups

    def bit(self, k):
        return rem(div(self.unit, 1 << k), 2)

    def partner(self, k):
        other = self.index + (1 - 2 * self.bit(k)) * (self.repeat << k)
        return {"blk": div(other, 2), "head": rem(other, 2)}

    def member(self, x, core, y):
        return {"blk": self.group * GROUP + 2 * x + core, "head": y}

    def beside(self, step):
        group = rem(self.group + self.groups + step, self.groups)
        return {"blk": group * GROUP + 2 * self.x + self.core, "head": self.y}

    def greet(self, cube=True, group=True, beside=True):
        barrier = pltpu.get_barrier_semaphore()
        partners = []
        if cube:
            partners += [self.partner(k) for k in range(5)]
        if group:
            partners += [
                self.member(
                    rem(self.x + dx, 2), rem(self.core + dc, 2), rem(self.y + dy, 2)
                )
                for dx in range(2)
                for dc in range(2)
                for dy in range(2)
                if dx + dc + dy
            ]
        if beside:
            partners += [self.beside(1), self.beside(-1)]
        for partner in partners:
            pl.semaphore_signal(barrier, inc=1, device_id=partner, device_id_type=MESH)
        pl.semaphore_wait(barrier, len(partners))


def remote(src, dst, send, recv, device):
    return pltpu.make_async_remote_copy(
        src_ref=src, dst_ref=dst, send_sem=send, recv_sem=recv, device_id=device, device_id_type=MESH
    )


class Pieces:
    def __init__(self, place, ref, rows, first, width, order, by_columns):
        self.place, self.ref, self.rows, self.first, self.width = place, ref, rows, first, width
        self.order, self.by_columns = order, by_columns
        self.shape = (rows, width // 2) if by_columns else (rows // 2, width)
        self.deltas = [(1 - 2 * place.bit(k)) * (1 << k) for k in order]

    def unit_of(self, mask, base=0):
        unit = self.place.unit
        for at in range(5):
            if isinstance(mask, int):
                if mask >> at & 1:
                    unit = unit + self.deltas[at]
            else:
                unit = unit + rem(div(mask, 1 << at), 2) * self.deltas[at]
        return unit

    def region(self, unit):
        slab, half = div(unit, 2), rem(unit, 2)
        if self.by_columns:
            return (
                rows_at(slab * self.rows, self.rows),
                rows_at(self.first + half * self.shape[1], self.shape[1], 128),
            )
        return (rows_at(unit * self.shape[0], self.shape[0]), pl.ds(self.first, self.width))

    def piece(self, mask):
        return self.ref.at[self.region(self.unit_of(mask))]


class Gather(Pieces):
    def begin(self, send, recv):
        self.send, self.recv = send, recv
        self.feed(0, 0)

    def copy(self, phase, mask, arriving=False):
        at = (1 << phase) - 1 + mask
        ref = self.piece(mask + (1 << phase) if arriving else mask)
        return remote(ref, ref, self.send.at[at], self.recv.at[at], self.place.partner(self.order[phase]))

    def feed(self, mask, phase):
        for later in range(phase, 5):
            self.copy(later, mask).start()

    def step(self, phase):
        def one(mask, carry):
            self.copy(phase, mask, True).wait_recv()
            self.feed(mask + (1 << phase), phase + 1)
            return carry

        lax.fori_loop(0, 1 << phase, one, 0)

    def finish(self):
        for phase in range(5):

            def one(mask, carry, phase=phase):
                self.copy(phase, mask).wait_send()
                return carry

            lax.fori_loop(0, 1 << phase, one, 0)


class Scatter(Pieces):
    def begin(self, landing, send, recv):
        self.landing, self.send, self.recv = landing, send, recv

        def one(j, carry):
            self.copy(0, j).start()
            return carry

        lax.fori_loop(0, 16, one, 0)

    def copy(self, phase, j):
        at = 32 - (1 << (5 - phase)) + j
        mask = (2 * j + 1) * (1 << phase)
        return remote(
            self.piece(mask),
            self.landing.at[at],
            self.send.at[at],
            self.recv.at[at],
            self.place.partner(self.order[phase]),
        )

    def absorb(self, phase, j):
        self.copy(phase, j).wait_recv()
        at = 32 - (1 << (5 - phase)) + j
        rows, columns = self.region(self.unit_of(j * (2 << phase)))
        total = self.ref[rows, columns].astype(F32) + self.landing[at].astype(F32)
        self.ref[rows, columns] = total.astype(BF16)
        return total

    def step(self, phase):
        half = 1 << (3 - phase)

        def odd(jj, carry):
            self.absorb(phase, 2 * jj + 1)
            self.copy(phase + 1, jj).start()
            return carry

        def even(jj, carry):
            self.absorb(phase, 2 * jj)
            return carry

        lax.fori_loop(0, half, odd, 0)
        lax.fori_loop(0, half, even, 0)

    def last(self):
        return self.absorb(4, 0)

    def finish(self):
        for phase in range(5):

            def one(j, carry, phase=phase):
                self.copy(phase, j).wait_send()
                return carry

            lax.fori_loop(0, 1 << (4 - phase), one, 0)


def to_heads(place, packed, landed, send, recv):
    tok = packed.shape[1]
    mine = rows_at(2 * tok * place.core + tok * place.y, tok)
    slot = 2 * place.core + place.y
    alone = place.core == place.x
    for dx in range(2):
        for dy in range(2):
            tx, ty = rem(place.x + dx, 2), rem(place.y + dy, 2)
            copy = remote(
                packed.at[2 * tx + ty],
                landed.at[mine],
                send.at[2 * dx + dy],
                recv.at[slot],
                place.member(tx, place.x, ty),
            )
            if dx + dy:
                copy.start()
            else:
                pl.when(jnp.logical_not(alone))(copy.start)

                @pl.when(alone)
                def _(tx=tx, ty=ty):
                    landed[mine] = packed[2 * tx + ty]


def to_heads_wait(place, packed, landed, send, recv):
    tok = packed.shape[1]
    alone = place.core == place.x
    for cs in range(2):
        for ys in range(2):
            part = landed.at[pl.ds(2 * tok * cs + tok * ys, tok)]
            copy = remote(part, part, send.at[0], recv.at[2 * cs + ys], place.member(place.x, 1 - place.core, place.y))
            own = alone & (place.core == cs) & (place.y == ys)
            pl.when(jnp.logical_not(own))(copy.wait_recv)


def to_heads_drain(place, packed, landed, send, recv):
    for at in range(4):
        copy = remote(packed.at[0], packed.at[0], send.at[at], recv.at[0], place.member(place.x, 1 - place.core, place.y))
        if at:
            copy.wait_send()
        else:
            pl.when(place.core != place.x)(copy.wait_send)


def to_tokens(place, rows, landed, send, recv):
    tok = landed.shape[1]
    chip = 2 * place.x + place.y
    for cs in range(2):
        for ys in range(2):
            part = pl.ds(2 * tok * cs + tok * ys, tok)
            own = (place.core == place.x) & (place.core == cs) & (place.y == ys)
            copy = remote(
                rows.at[part], landed.at[chip], send.at[2 * cs + ys], recv.at[chip], place.member(place.core, cs, ys)
            )
            pl.when(jnp.logical_not(own))(copy.start)

            @pl.when(own)
            def _(part=part):
                landed[chip] = rows[part]


def to_tokens_wait(place, rows, landed, send, recv):
    for xs in range(2):
        for ys in range(2):
            at = 2 * xs + ys
            own = (place.core == place.x) & (place.x == xs) & (place.y == ys)
            copy = remote(
                landed.at[at], landed.at[at], send.at[at], recv.at[at], place.member(place.x, 1 - place.core, place.y)
            )
            pl.when(jnp.logical_not(own))(copy.wait_recv)


def to_tokens_drain(place, rows, landed, send, recv):
    for cs in range(2):
        for ys in range(2):
            own = (place.core == place.x) & (place.core == cs) & (place.y == ys)
            at = 2 * cs + ys
            copy = remote(
                landed.at[at], landed.at[at], send.at[at], recv.at[at], place.member(place.x, 1 - place.core, place.y)
            )
            pl.when(jnp.logical_not(own))(copy.wait_send)


def spread_rows(small, per, width, keep):
    lane = lax.broadcasted_iota(jnp.int32, (128, width), 1).astype(F32)
    turn = jnp.floor((lane + 0.5) * (1.0 / per))
    place = lane - per * turn
    pick = (place == lax.broadcasted_iota(jnp.int32, (128, width), 0).astype(F32)).astype(BF16)
    wide = nn(small, pick)
    row = lax.broadcasted_iota(jnp.int32, wide.shape, 0)
    column = lax.broadcasted_iota(jnp.int32, wide.shape, 1)
    low = lax.shift_right_logical(row, 4 if keep is None else 0) * per
    wide = jnp.where((column >= low) & (column < low + per), wide, 0.0)
    if keep is None:
        return jnp.sum(wide.reshape(-1, 16, width), axis=0)
    return jnp.sum(wide, axis=0, keepdims=True)


AG_PLAN = dict(qkv=(4, 3, 2, 0, 1), out=(4, 3, 0, 2, 1), ff1=(4, 3, 0, 2, 1), ff2=(4, 3, 2, 0, 1))
RS_PLAN = dict(qkv=(1, 0, 2, 3, 4), out=(1, 2, 0, 3, 4), ff1=(1, 2, 0, 3, 4), ff2=(1, 0, 2, 3, 4))


def matrices(dim, ff):
    return (("qkv", 0, 3 * dim), ("out", 3 * dim, dim), ("ff1", 4 * dim, ff))


def enter_kernel(
    repeat, groups,
    shard3, shard_ff2, small, tokens,
    all3_out, ff2_out, params_out, ffb_out, q_out, kv_out,
    stage, all3, all_ff2, smalls, params, pack_q, pack_kv, q_rows, window,
    y_sems, small_send, small_recv, gather_send, gather_recv, q_send, q_recv,
    kv_send, kv_recv, near_send, near_recv, side_send, side_recv, local,
):
    place = Place(repeat, groups)
    dim, joined = all3.shape
    ff = all_ff2.shape[0]
    tok = tokens.shape[0]
    unit_rows = dim // 32
    slab = 2 * unit_rows
    own_ff2 = pltpu.make_async_copy(
        shard_ff2, all_ff2.at[rows_at(place.unit * (ff // 32), ff // 32)], local.at[0]
    )
    own_ff2.start()
    smalls[rows_at(place.unit * 16, 16)] = small[...]
    place.greet()
    cuts = matrices(dim, ff)
    y_copies = []
    def half_columns(at, half):
        name, first, width = cuts[at]
        return (slice(None), rows_at(first + half * (width // 2), width // 2, 128))

    for at in range(3):
        mine, other = half_columns(at, place.bit(0)), half_columns(at, 1 - place.bit(0))
        out = remote(shard3.at[other], stage.at[other], y_sems.at[at], y_sems.at[4 + at], place.partner(0))
        back = remote(shard3.at[mine], stage.at[mine], y_sems.at[at], y_sems.at[4 + at], place.partner(0))
        out.start()
        y_copies.append((out, back))

    def small_copy(phase):
        rows = rows_at(div(place.unit, 1 << phase) * (16 << phase), 16 << phase)
        other = div(place.unit, 1 << phase) + (1 - 2 * place.bit(phase))
        there = rows_at(other * (16 << phase), 16 << phase)
        return [
            remote(smalls.at[part], smalls.at[part], small_send.at[phase], small_recv.at[phase], place.partner(phase))
            for part in (rows, there)
        ]

    small_copy(0)[0].start()
    gathers = {
        name: Gather(place, all3, slab, first, width, AG_PLAN[name], True) for name, first, width in cuts
    }
    gathers["ff2"] = Gather(place, all_ff2, ff // 16, 0, dim, AG_PLAN["ff2"], False)
    here = rows_at(div(place.unit, 2) * slab, slab)

    def merge(at):
        y_copies[at][1].wait_recv()
        name, first, width = cuts[at]
        low = place.bit(0) == 0
        for column in range(0, width // 2, 384):
            part = rows_at(first + place.bit(0) * (width // 2) + column, 384, 128)
            mine, other = shard3[:unit_rows, part].astype(F32), stage[:unit_rows, part].astype(F32)
            whole = jnp.concatenate([jnp.where(low, mine, other), jnp.where(low, other, mine)], axis=0)
            all3[here, part] = whole.astype(BF16)
        gathers[name].begin(gather_send.at[at], gather_recv.at[at])

    merge(0)
    own_ff2.wait()
    gathers["ff2"].begin(gather_send.at[3], gather_recv.at[3])
    merge(2)
    merge(1)
    for phase in range(5):
        small_copy(phase)[1].wait_recv()
        if phase < 4:
            small_copy(phase + 1)[0].start()
        gathers["qkv"].step(phase)
        if phase < 2:
            for name in ("ff2", "ff1", "out"):
                gathers[name].step(phase)
    params[...] = spread_rows(smalls[...], unit_rows, dim, None)
    rows16 = lax.broadcasted_iota(jnp.int32, (32, 512), 0) * 16 + 8
    chosen = (rows16 == lax.broadcasted_iota(jnp.int32, (32, 512), 1)).astype(BF16)
    ffb_out[...] = jnp.broadcast_to(
        spread_rows(nn(chosen, smalls[...]).astype(BF16), ff // 32, ff, 0), ffb_out.shape
    )
    params_out[...] = params[...]
    rows = tokens[...]
    values = []
    for part, bias in ((0, 4), (1, None), (2, 5)):
        made = nn(rows, all3[:, part * dim:(part + 1) * dim])
        if bias is not None:
            made = made + params[bias:bias + 1, :]
        values.append(made)
    for chip in range(CHIPS):
        cut = slice(HW * chip, HW * (chip + 1))
        pack_kv[chip] = jnp.concatenate([values[1][:, cut], values[2][:, cut]], axis=1).astype(BF16)
    mine = rows_at(4 * tok * place.x + 2 * tok * place.core + tok * place.y, tok)

    def kv_copy(dx, dy):
        tx, ty = rem(place.x + dx, 2), rem(place.y + dy, 2)
        at = 2 * dx + dy
        src = pack_kv.at[2 * tx + ty]
        out = remote(src, window.at[1].at[mine], kv_send.at[at], kv_recv.at[at], place.member(tx, place.core, ty))
        there = rows_at(4 * tok * tx + 2 * tok * place.core + tok * ty, tok)
        back = remote(src, window.at[1].at[there], kv_send.at[at], kv_recv.at[at], place.member(tx, place.core, ty))
        return out, back

    for dx, dy in ((1, 1), (1, 0), (0, 1)):
        kv_copy(dx, dy)[0].start()
    window[1, mine] = pack_kv[2 * place.x + place.y]
    for chip in range(CHIPS):
        cut = slice(HW * chip, HW * (chip + 1))
        pack_q[chip] = jnp.concatenate([values[0][:, cut], jnp.zeros((tok, QW - HW), F32)], axis=1).astype(BF16)
    to_heads(place, pack_q, q_rows, q_send, q_recv)

    sibling = place.member(place.x, 1 - place.core, place.y)

    def stretch(slot, half, core):
        return window.at[slot].at[rows_at(4 * tok * half + 2 * tok * core, 2 * tok)]

    def near(slot, half, arriving=False):
        ref = stretch(slot, half, 1 - place.core if arriving else place.core)
        at = 2 * slot + half
        return remote(ref, ref, near_send.at[at], near_recv.at[at], sibling)

    def side(step, half):
        at = (1 - step) + half
        return remote(
            stretch(1, half, place.core), stretch(1 - step, half, place.core), side_send.at[at], side_recv.at[at],
            place.beside(step),
        )

    for dx, dy in ((1, 1), (1, 0), (0, 1)):
        kv_copy(dx, dy)[1].wait_recv()
    for half in range(2):
        for step in (1, -1):
            side(step, half).start()
    for half in range(2):
        near(1, half).start()
    for phase in range(2, 5):
        for name in ("ff2", "ff1", "out"):
            gathers[name].step(phase)
    for gather in gathers.values():
        gather.finish()
    copies = [
        pltpu.make_async_copy(all3, all3_out, local.at[0]),
        pltpu.make_async_copy(all_ff2, ff2_out, local.at[1]),
    ]
    for copy in copies:
        copy.start()
    for half in range(2):
        for step in (1, -1):
            side(step, half).wait_recv()
            near(1 - step, half).start()
    for slot in range(3):
        for half in range(2):
            near(slot, half, True).wait_recv()
    to_heads_wait(place, pack_q, q_rows, q_send, q_recv)
    last = [
        pltpu.make_async_copy(q_rows, q_out, local.at[2]),
        pltpu.make_async_copy(window, kv_out, local.at[3]),
    ]
    for copy in last:
        copy.start()
    for out, back in y_copies:
        out.wait_send()
    for phase in range(5):
        small_copy(phase)[0].wait_send()
    for dx, dy in ((1, 1), (1, 0), (0, 1)):
        kv_copy(dx, dy)[0].wait_send()
    for half in range(2):
        for step in (1, -1):
            side(step, half).wait_send()
        for slot in range(3):
            near(slot, half).wait_send()
    to_heads_drain(place, pack_q, q_rows, q_send, q_recv)
    for copy in copies + last:
        copy.wait()


VM = pl.BlockSpec(memory_space=pltpu.VMEM)
HBM = pl.BlockSpec(memory_space=pl.ANY)
DMA = pltpu.SemaphoreType.DMA


def enter(repeat, groups, shard3, shard_ff2, small, tokens):
    tok, dim = tokens.shape
    joined = shard3.shape[1]
    ff = shard_ff2.shape[0] * 32
    shape = jax.ShapeDtypeStruct
    return pl.pallas_call(
        functools.partial(enter_kernel, repeat, groups),
        out_shape=(
            shape((dim, joined), BF16), shape((ff, dim), BF16), shape((16, dim), F32), shape((8, ff), F32),
            shape((4 * tok, QW), BF16), shape((3, 8 * tok, KW), BF16),
        ),
        in_specs=[VM] * 4,
        out_specs=(HBM, HBM, VM, VM, HBM, HBM),
        scratch_shapes=[
            pltpu.VMEM(shard3.shape, BF16), pltpu.VMEM((dim, joined), BF16), pltpu.VMEM((ff, dim), BF16),
            pltpu.VMEM((512, 128), BF16), pltpu.VMEM((16, dim), F32),
            pltpu.VMEM((CHIPS, tok, QW), BF16), pltpu.VMEM((CHIPS, tok, KW), BF16),
            pltpu.VMEM((4 * tok, QW), BF16), pltpu.VMEM((3, 8 * tok, KW), BF16),
            DMA((8,)), DMA((5,)), DMA((5,)), DMA((4, 31)), DMA((4, 31)), DMA((4,)), DMA((4,)),
            DMA((4,)), DMA((4,)), DMA((6,)), DMA((6,)), DMA((4,)), DMA((4,)), DMA((4,)),
        ],
        compiler_params=pltpu.CompilerParams(
            collective_id=1, has_side_effects=True, vmem_limit_bytes=VMEM_BYTES
        ),
    )(shard3, shard_ff2, small, tokens)


def pack_small(norm_gains, norm_biases, proj_biases, ff_bias):
    rows = jnp.concatenate([norm_gains, norm_biases, proj_biases], axis=0)
    rows = jnp.pad(rows, ((0, 0), (0, 128 - rows.shape[1])))
    hidden = jnp.pad(ff_bias, (0, 128 - ff_bias.shape[0]))[None]
    return jnp.concatenate([rows, hidden, jnp.zeros((7, 128), rows.dtype)], axis=0)


QT = 512
KT = 512


def lane_mask(shape, low, high, axis):
    lane = lax.broadcasted_iota(jnp.int32, shape, axis)
    return (lane >= low) & (lane < high)


HEAD_QUERY = ((0, 0), (0, 64), (128, 0))
HEAD_VALUE = ((128, 64), (256, 0), (256, 64))
HEAD_CONTEXT = ((0, 64), (128, 0), (128, 64))


def head_rows(ref, rows, spot):
    tile, place = spot
    part = ref[rows, tile:tile + 128]
    return jnp.where(lane_mask(part.shape, place, place + HD, 1), part, jnp.zeros_like(part))


def forward_kernel(bounds, queries, window, query_ids, key_ids, context_out, sums_out):
    count = queries.shape[0]
    scale = HD ** (-0.5)

    def tile(at, carry):
        rows = rows_at(at * QT, QT)
        ids = query_ids[0:1, rows_at(at * QT, QT, 128)]
        parts = []
        scaled = [head_rows(queries, rows, HEAD_QUERY[head]) * jnp.asarray(scale, BF16) for head in range(3)]

        def visit(j, state):
            keys = rows_at(j * KT, KT)
            allowed = jnp.concatenate([key_ids[keys, :]] * (QT // 128), axis=1) == ids
            tops, terms, fresh = [], [], []
            scores = [
                jnp.where(allowed, nt(window[keys, tile_at:tile_at + 128], scaled[head]), NEGATIVE)
                for head, (tile_at, place) in enumerate(HEAD_QUERY)
            ]
            for head in range(3):
                tops.append(jnp.maximum(state[3 * head], jnp.max(scores[head], axis=0, keepdims=True)))
            for head in range(3):
                terms.append(jnp.exp(scores[head] - tops[head]))
            for head in range(3):
                highest, total, weighted = state[3 * head:3 * head + 3]
                tile_at = HEAD_VALUE[head][0]
                factor = jnp.exp(highest - tops[head])
                total = total * factor + jnp.sum(terms[head], axis=0, keepdims=True)
                weighted = weighted * factor + tn(window[keys, tile_at:tile_at + 128], terms[head].astype(BF16))
                fresh += [tops[head], total, weighted]
            return tuple(fresh)

        start = []
        for head in range(3):
            start += [jnp.full((1, QT), NEGATIVE, F32), jnp.zeros((1, QT), F32), jnp.zeros((128, QT), F32)]
        state = lax.fori_loop(bounds[0, at], bounds[1, at], visit, tuple(start))
        made = []
        for head in range(3):
            highest, total, weighted = state[3 * head:3 * head + 3]
            whole = weighted / total
            place = HEAD_CONTEXT[head][1]
            made.append(jnp.where(lane_mask(whole.shape, place, place + HD, 0), whole, 0.0))
            sums_out[head:head + 1, rows_at(at * QT, QT, 128)] = highest + jnp.log(total)
        context_out[rows, 0:128] = made[0].T
        context_out[rows, 128:256] = (made[1] + made[2]).T
        return carry

    lax.fori_loop(0, count // QT, tile, 0)


SM = pl.BlockSpec(memory_space=pltpu.SMEM)


def forward(bounds, queries, window, query_ids, key_ids):
    count = queries.shape[0]
    shape = jax.ShapeDtypeStruct
    return pl.pallas_call(
        forward_kernel,
        out_shape=(shape((count, QW), F32), shape((8, count), F32)),
        in_specs=[SM] + [VM] * 4,
        out_specs=(VM, VM),
        compiler_params=pltpu.CompilerParams(vmem_limit_bytes=VMEM_BYTES),
    )(bounds, queries, window, query_ids, key_ids)


def backward_kernel(bounds, queries, window, query_ids, key_ids, context, grads, sums, query_out, window_out, acc):
    count = queries.shape[0]
    scale = HD ** (-0.5)
    acc[...] = jnp.zeros_like(acc)

    def tile(at, carry):
        rows = rows_at(at * QT, QT)
        ids = query_ids[0:1, rows_at(at * QT, QT, 128)]
        scaled, grad, delta, sum_rows = [], [], [], []
        for head in range(3):
            scaled.append(head_rows(queries, rows, HEAD_QUERY[head]) * jnp.asarray(scale, BF16))
            mine = head_rows(grads, rows, HEAD_CONTEXT[head])
            tile_at = HEAD_CONTEXT[head][0]
            product = mine.astype(F32) * context[rows, tile_at:tile_at + 128]
            grad.append(mine)
            delta.append(
                lax.dot_general(
                    jnp.ones((8, 128), F32), product, (((1,), (1,)), ((), ())),
                    precision=lax.Precision.HIGHEST, preferred_element_type=F32,
                )[0:1]
            )
            sum_rows.append(sums[head:head + 1, rows_at(at * QT, QT, 128)])

        def visit(j, state):
            keys = rows_at(j * KT, KT)
            allowed = jnp.concatenate([key_ids[keys, :]] * (QT // 128), axis=1) == ids
            fresh, key_grads, value_grads = [], [], []
            for head in range(3):
                key = window[keys, HEAD_QUERY[head][0]:HEAD_QUERY[head][0] + 128]
                value = window[keys, HEAD_VALUE[head][0]:HEAD_VALUE[head][0] + 128]
                probs = jnp.where(allowed, jnp.exp(nt(key, scaled[head]) - sum_rows[head]), 0.0)
                spread = nt(value, grad[head])
                steps = (probs * (spread - delta[head])).astype(BF16)
                value_grads.append(nn(probs.astype(BF16), grad[head]))
                key_grads.append(nn(steps, scaled[head]))
                fresh.append(state[head] + tn(key, steps))
            acc[keys, 0:128] += key_grads[0] + key_grads[1]
            acc[keys, 128:256] += key_grads[2] + value_grads[0]
            acc[keys, 256:384] += value_grads[1] + value_grads[2]
            return tuple(fresh)

        state = lax.fori_loop(
            bounds[0, at], bounds[1, at], visit, tuple(jnp.zeros((128, QT), F32) for _ in range(3))
        )
        made = []
        for head in range(3):
            place = HEAD_QUERY[head][1]
            made.append(jnp.where(lane_mask(state[head].shape, place, place + HD, 0), state[head] * scale, 0.0))
        query_out[rows, 0:128] = (made[0] + made[1]).T.astype(BF16)
        query_out[rows, 128:256] = made[2].T.astype(BF16)
        return carry

    lax.fori_loop(0, count // QT, tile, 0)

    def store(at, carry):
        rows = rows_at(at * KT, KT)
        window_out[rows, :] = acc[rows, :].astype(BF16)
        return carry

    lax.fori_loop(0, acc.shape[0] // KT, store, 0)


def backward(bounds, queries, window, query_ids, key_ids, context, grads, sums):
    shape = jax.ShapeDtypeStruct
    return pl.pallas_call(
        backward_kernel,
        out_shape=(shape(queries.shape, BF16), shape(window.shape, BF16)),
        in_specs=[SM] + [VM] * 7,
        out_specs=(VM, VM),
        scratch_shapes=[pltpu.VMEM(window.shape, F32)],
        compiler_params=pltpu.CompilerParams(vmem_limit_bytes=VMEM_BYTES),
    )(bounds, queries, window, query_ids, key_ids, context, grads, sums)


def doc_tables(doc_starts, core, group, half_rows, total_rows):
    window = 6 * half_rows
    live = jnp.sum((doc_starts < total_rows).astype(jnp.int32))

    def ids(places):
        return lax.rem(jnp.sum((doc_starts[None, :] <= places[:, None]).astype(jnp.int32), axis=1), live)

    start = group * 2 * half_rows
    key_ids = ids(jnp.mod(start - 2 * half_rows + jnp.arange(window, dtype=jnp.int32), total_rows))
    query_ids = lax.dynamic_slice_in_dim(key_ids, 2 * half_rows + core * half_rows, half_rows)
    tiles = query_ids.reshape(-1, QT)
    keys = key_ids.reshape(1, -1, KT)

    def any_tile(edge):
        return jnp.any(keys == edge[:, None, None], axis=2)

    order = jnp.arange(window // KT, dtype=jnp.int32)[None]
    low = jnp.min(jnp.where(any_tile(tiles[:, 0]), order, window), axis=1)
    high = jnp.max(jnp.where(any_tile(tiles[:, -1]), order + 1, 0), axis=1)
    return (
        jnp.stack([low, high]),
        jnp.broadcast_to(query_ids[None], (8, half_rows)),
        jnp.broadcast_to(key_ids[:, None], (window, 128)),
    )


def norm_forward(values):
    center = values - jnp.mean(values, axis=-1, keepdims=True)
    scale = lax.rsqrt(jnp.mean(center * center, axis=-1, keepdims=True) + EPSILON)
    return center * scale, scale


def norm_backward(grad, unit_rows, scale, gain):
    inner = grad * gain
    gain_row = jnp.sum(grad * unit_rows, axis=0, keepdims=True)
    shift_row = jnp.sum(grad, axis=0, keepdims=True)
    back = scale * (
        inner
        - jnp.mean(inner, axis=-1, keepdims=True)
        - unit_rows * jnp.mean(inner * unit_rows, axis=-1, keepdims=True)
    )
    return back, gain_row, shift_row


def column_sum(values):
    return jnp.sum(values.astype(F32), axis=0, keepdims=True)


def middle_kernel(
    repeat, groups,
    context, tokens, d_out, params, ffb, all3, all_ff2,
    out, d_mid_out, grads_out, grad_o3, grad_ff2, sum_rows,
    w_out, w_ff1, w_ff2, ctx_rows, parts, pack, grad_rows, act, slope, d_pre,
    send, recv, back_send, back_recv, local,
):
    place = Place(repeat, groups)
    tok, dim = tokens.shape
    ff = w_ff1.shape[1]
    loads = [
        pltpu.make_async_copy(all3.at[:, pl.ds(3 * dim, dim)], w_out, local.at[0]),
        pltpu.make_async_copy(all3.at[:, pl.ds(4 * dim, ff)], w_ff1, local.at[1]),
        pltpu.make_async_copy(all_ff2, w_ff2, local.at[2]),
    ]
    for load in loads:
        load.start()
    ctx_rows[...] = context[...].astype(BF16)
    place.greet(cube=False, beside=False)
    to_tokens(place, ctx_rows, parts, send, recv)
    to_tokens_wait(place, ctx_rows, parts, send, recv)
    joined = jnp.concatenate([parts[chip][:, QW - HW:].astype(F32) for chip in range(CHIPS)], axis=1).astype(BF16)
    loads[0].wait()
    gains, shifts = [params[at:at + 1, :] for at in (0, 1)], [params[at:at + 1, :] for at in (2, 3)]
    mid = tokens[...].astype(F32) + (nn(joined, w_out[...]) + params[6:7, :])
    unit_first, scale_first = norm_forward(mid)
    hidden = unit_first * gains[0] + shifts[0]
    low = hidden.astype(BF16)
    loads[1].wait()
    loads[2].wait()
    ff_out = jnp.zeros((tok, dim), F32)
    for first in range(0, ff, dim):
        cut = slice(first, first + dim)
        pre = nn(low, w_ff1[:, cut]) + ffb[0:1, cut]
        bell = 0.5 * (1.0 + lax.erf(pre * 0.7071067811865476))
        made = (pre * bell).astype(BF16)
        act[:, cut] = made
        slope[:, cut] = bell + pre * jnp.exp(-0.5 * pre * pre) * 0.3989422804014327
        ff_out = ff_out + nn(made, w_ff2[cut, :])
    unit_second, scale_second = norm_forward(hidden + (ff_out + params[7:8, :]))
    out[...] = (unit_second * gains[1] + shifts[1]).astype(BF16)
    d_sum, gain_second, shift_second = norm_backward(d_out[...].astype(F32), unit_second, scale_second, gains[1])
    d_ff = d_sum.astype(BF16)
    d_hidden = d_sum
    for first in range(0, ff, dim):
        cut = slice(first, first + dim)
        made = (nt(d_ff, w_ff2[cut, :]) * slope[:, cut]).astype(BF16)
        d_pre[:, cut] = made
        d_hidden = d_hidden + nt(made, w_ff1[:, cut])
    d_mid, gain_first, shift_first = norm_backward(d_hidden, unit_first, scale_first, gains[0])
    d_mid_out[...] = d_mid
    d_attn = d_mid.astype(BF16)
    d_context = nt(d_attn, w_out[...])
    for chip in range(CHIPS):
        pack[chip] = jnp.concatenate(
            [jnp.zeros((tok, QW - HW), F32), d_context[:, HW * chip:HW * (chip + 1)]], axis=1
        ).astype(BF16)
    to_heads(place, pack, grad_rows, back_send, back_recv)
    for first in range(0, ff, dim):
        cut = slice(first, first + dim)
        grad_ff2[cut, :] = tn(act[:, cut], d_ff).astype(BF16)
        grad_o3[:, dim + first:2 * dim + first] = tn(low, d_pre[:, cut]).astype(BF16)
        sum_rows[8 + first // dim:9 + first // dim, :] = column_sum(d_pre[:, cut])
    grad_o3[:, 0:dim] = tn(joined, d_attn).astype(BF16)
    for at, row in enumerate(
        (
            gain_first, gain_second, shift_first, shift_second,
            jnp.zeros((1, dim), F32), jnp.zeros((1, dim), F32), column_sum(d_attn), column_sum(d_ff),
        )
    ):
        sum_rows[at:at + 1, :] = row
    sum_rows[8 + ff // dim:, :] = jnp.zeros((8 - ff // dim, dim), F32)
    to_heads_wait(place, pack, grad_rows, back_send, back_recv)
    grads_out[...] = grad_rows[...]
    to_tokens_drain(place, ctx_rows, parts, send, recv)
    to_heads_drain(place, pack, grad_rows, back_send, back_recv)


def middle(repeat, groups, context, tokens, d_out, params, ffb, all3, all_ff2):
    tok, dim = tokens.shape
    ff = all_ff2.shape[0]
    shape = jax.ShapeDtypeStruct
    vm = pltpu.VMEM
    return pl.pallas_call(
        functools.partial(middle_kernel, repeat, groups),
        out_shape=(
            shape((tok, dim), BF16), shape((tok, dim), F32), shape((4 * tok, QW), BF16),
            shape((dim, dim + ff), BF16), shape((ff, dim), BF16), shape((16, dim), F32),
        ),
        in_specs=[VM] * 5 + [HBM] * 2,
        out_specs=(VM,) * 6,
        scratch_shapes=[
            vm((dim, dim), BF16), vm((dim, ff), BF16), vm((ff, dim), BF16), vm((4 * tok, QW), BF16),
            vm((CHIPS, tok, QW), BF16), vm((CHIPS, tok, QW), BF16), vm((4 * tok, QW), BF16),
            vm((tok, ff), BF16), vm((tok, ff), F32), vm((tok, ff), BF16),
            DMA((4,)), DMA((4,)), DMA((4,)), DMA((4,)), DMA((4,)),
        ],
        compiler_params=pltpu.CompilerParams(collective_id=2, has_side_effects=True, vmem_limit_bytes=VMEM_BYTES),
    )(context, tokens, d_out, params, ffb, all3, all_ff2)


def leave_kernel(
    repeat, groups,
    d_query, d_window, tokens, d_mid, sum_rows, all3, grad_o3, grad_ff2_in,
    d_tokens, g_qkv, g_out, g_ff1, g_ff2, g_rows,
    w_qkv, grad3, grad_ff2, land_qkv, land_out, land_ff1, land_ff2,
    near_land, side_land, stretch_sum, kv_parts, q_parts, joined, swap_out, swap_in, rows_mine, rows_land,
    grad_send, grad_recv, near_send, near_recv, side_send, side_recv, kv_send, kv_recv,
    q_send, q_recv, swap_send, swap_recv, rows_send, rows_recv, local,
):
    place = Place(repeat, groups)
    tok, dim = tokens.shape
    ff = grad_ff2.shape[0]
    unit_rows = dim // 32
    loads = [
        pltpu.make_async_copy(grad_o3, grad3.at[:, pl.ds(3 * dim, dim + ff)], local.at[0]),
        pltpu.make_async_copy(grad_ff2_in, grad_ff2, local.at[1]),
        pltpu.make_async_copy(all3.at[:, pl.ds(0, 3 * dim)], w_qkv, local.at[2]),
    ]
    for load in loads:
        load.start()
    place.greet()
    sibling = place.member(place.x, 1 - place.core, place.y)

    def stretch(slot, half, core):
        return rows_at(4 * tok * half + 2 * tok * core, 2 * tok)

    def near(slot, half):
        at = 2 * slot + half
        return remote(
            d_window.at[slot].at[stretch(slot, half, 1 - place.core)], near_land.at[at],
            near_send.at[at], near_recv.at[at], sibling,
        )

    order = (0, 2, 1)
    for slot in order:
        for half in range(2):
            near(slot, half).start()
    to_tokens(place, d_query, q_parts, q_send, q_recv)
    cuts = matrices(dim, ff)
    slab = 2 * unit_rows
    scatters = {
        name: Scatter(place, grad3, slab, first, width, RS_PLAN[name], True) for name, first, width in cuts
    }
    scatters["ff2"] = Scatter(place, grad_ff2, ff // 16, 0, dim, RS_PLAN["ff2"], False)
    lands = dict(qkv=land_qkv, out=land_out, ff1=land_ff1, ff2=land_ff2)

    def begin(name, at):
        scatters[name].begin(lands[name], grad_send.at[at], grad_recv.at[at])

    def side(slot, half):
        at = slot + half
        return remote(
            stretch_sum.at[at], side_land.at[at], side_send.at[at], side_recv.at[at],
            place.beside(-1 if slot == 0 else 1),
        )

    def add_near(slot, half, target):
        near(slot, half).wait_recv()
        at = 2 * slot + half
        mine = d_window[slot, stretch(slot, half, place.core)].astype(F32) + near_land[at].astype(F32)
        target[...] = mine.astype(BF16)

    loads[0].wait()
    loads[1].wait()
    begin("ff2", 3)
    for slot in (0, 2):
        for half in range(2):
            add_near(slot, half, stretch_sum.at[slot + half])
            side(slot, half).start()
    begin("ff1", 2)
    begin("out", 1)
    for phase in range(2):
        for name in ("ff2", "ff1", "out"):
            scatters[name].step(phase)

    def kv_copy(dx, dy):
        tx, ty = rem(place.x + dx, 2), rem(place.y + dy, 2)
        at = 2 * dx + dy
        return remote(
            stretch_sum.at[4 + tx].at[rows_at(tok * ty, tok)], kv_parts.at[2 * place.x + place.y],
            kv_send.at[at], kv_recv.at[at], place.member(tx, place.core, ty),
        )

    for half in range(2):
        near(1, half).wait_recv()
        at = 2 + half
        total = d_window[1, stretch(1, half, place.core)].astype(F32) + near_land[at].astype(F32)
        for slot in (0, 2):
            side(slot, half).wait_recv()
            total = total + side_land[slot + half].astype(F32)
        stretch_sum[4 + half] = total.astype(BF16)
    for dx, dy in ((1, 1), (1, 0), (0, 1)):
        kv_copy(dx, dy).start()
    kv_parts[2 * place.x + place.y] = stretch_sum[4 + place.x, rows_at(tok * place.y, tok)]
    to_tokens_wait(place, d_query, q_parts, q_send, q_recv)
    joined[:, 0:dim] = jnp.concatenate(
        [q_parts[chip][:, :HW].astype(F32) for chip in range(CHIPS)], axis=1
    ).astype(BF16)
    for dx, dy in ((1, 1), (1, 0), (0, 1)):
        kv_copy(dx, dy).wait_recv()
    for at in range(2):
        joined[:, (1 + at) * dim:(2 + at) * dim] = jnp.concatenate(
            [kv_parts[chip][:, HW * at:HW * (at + 1)].astype(F32) for chip in range(CHIPS)], axis=1
        ).astype(BF16)
    for part in range(3):
        cut = slice(part * dim, (part + 1) * dim)
        grad3[:, cut] = tn(tokens[...], joined[:, cut]).astype(BF16)
    begin("qkv", 0)
    rows_mine[0] = sum_rows[...]
    rows_mine[0, 4:5, :] = column_sum(joined[:, 0:dim])
    rows_mine[0, 5:6, :] = column_sum(joined[:, 2 * dim:3 * dim])

    def rows_copy(phase):
        return remote(
            rows_mine.at[phase], rows_land.at[phase], rows_send.at[phase], rows_recv.at[phase], place.partner(phase)
        )

    def rows_add(phase):
        rows_copy(phase).wait_recv()
        rows_mine[phase + 1] = rows_mine[phase] + rows_land[phase]
        if phase < 4:
            rows_copy(phase + 1).start()

    rows_copy(0).start()

    def swap(at):
        name, first, width = cuts[at]
        part = (slice(None), pl.ds(first // 2, width // 2))
        return remote(swap_out.at[part], swap_in.at[part], swap_send.at[at], swap_recv.at[at], place.partner(0))

    def finish_half(at):
        name, first, width = cuts[at]
        target = (g_qkv, g_out, g_ff1)[at]
        total = scatters[name].last()
        high = place.bit(0) == 1
        keep = jnp.where(high, total[unit_rows:], total[:unit_rows])
        give = jnp.where(high, total[:unit_rows], total[unit_rows:])
        pad = jnp.zeros((swap_out.shape[0] - unit_rows, give.shape[1]), F32)
        swap_out[:, first // 2:(first + width) // 2] = jnp.concatenate([give, pad], axis=0).astype(BF16)
        swap(at).start()
        target[:, rows_at(place.bit(0) * (width // 2), width // 2, 128)] = keep

    def finish_swap(at):
        name, first, width = cuts[at]
        target = (g_qkv, g_out, g_ff1)[at]
        swap(at).wait_recv()
        other = swap_in[:, first // 2:(first + width) // 2].astype(F32)[:unit_rows]
        target[:, rows_at((1 - place.bit(0)) * (width // 2), width // 2, 128)] = other

    loads[2].wait()
    d_tokens[...] = (d_mid[...] + nt(joined[...], w_qkv[...])).astype(BF16)
    for phase in range(4):
        if phase >= 2:
            for name in ("ff2", "ff1", "out"):
                scatters[name].step(phase)
        scatters["qkv"].step(phase)
        rows_add(phase)
    rows_add(4)
    g_ff2[...] = scatters["ff2"].last()
    for at in (2, 1, 0):
        finish_half(at)
    for at in (2, 1, 0):
        finish_swap(at)
    g_rows[...] = rows_mine[5]
    for phase in range(5):
        rows_copy(phase).wait_send()
    for scatter in scatters.values():
        scatter.finish()
    for at in range(3):
        swap(at).wait_send()
    for slot in range(3):
        for half in range(2):
            near(slot, half).wait_send()
    for slot in (0, 2):
        for half in range(2):
            side(slot, half).wait_send()
    for dx, dy in ((1, 1), (1, 0), (0, 1)):
        kv_copy(dx, dy).wait_send()
    to_tokens_drain(place, d_query, q_parts, q_send, q_recv)


def leave(repeat, groups, d_query, d_window, tokens, d_mid, sum_rows, all3, grad_o3, grad_ff2):
    tok, dim = tokens.shape
    ff = grad_ff2.shape[0]
    unit = dim // 32
    slab = 2 * unit
    shape = jax.ShapeDtypeStruct
    vm = pltpu.VMEM
    return pl.pallas_call(
        functools.partial(leave_kernel, repeat, groups),
        out_shape=(
            shape((tok, dim), BF16), shape((unit, 3 * dim), F32), shape((unit, dim), F32), shape((unit, ff), F32),
            shape((ff // 32, dim), F32), shape((16, dim), F32),
        ),
        in_specs=[VM] * 5 + [HBM] * 3,
        out_specs=(VM,) * 6,
        scratch_shapes=[
            vm((dim, 3 * dim), BF16), vm((dim, 4 * dim + ff), BF16), vm((ff, dim), BF16),
            vm((31, slab, 3 * dim // 2), BF16), vm((31, slab, dim // 2), BF16), vm((31, slab, ff // 2), BF16),
            vm((31, ff // 32, dim), BF16),
            vm((6, 2 * tok, KW), BF16), vm((4, 2 * tok, KW), BF16), vm((6, 2 * tok, KW), BF16),
            vm((CHIPS, tok, KW), BF16), vm((CHIPS, tok, QW), BF16), vm((tok, 3 * dim), BF16),
            vm((-(-unit // 16) * 16, (4 * dim + ff) // 2), BF16), vm((-(-unit // 16) * 16, (4 * dim + ff) // 2), BF16),
            vm((6, 16, dim), F32), vm((5, 16, dim), F32),
            DMA((4, 31)), DMA((4, 31)), DMA((6,)), DMA((6,)), DMA((4,)), DMA((4,)), DMA((4,)), DMA((4,)),
            DMA((4,)), DMA((4,)), DMA((3,)), DMA((3,)), DMA((5,)), DMA((5,)), DMA((3,)),
        ],
        compiler_params=pltpu.CompilerParams(collective_id=3, has_side_effects=True, vmem_limit_bytes=VMEM_BYTES),
    )(d_query, d_window, tokens, d_mid, sum_rows, all3, grad_o3, grad_ff2)


def gather_repeat(value, repeat, axis):
    if repeat == 1:
        return value
    count = repeat // 2
    sets = [list(range(at, at + count)) for at in range(0, lax.axis_size("blk"), count)]
    value = lax.all_gather(value, "head", axis=axis, tiled=True)
    if count == 1:
        return value
    return lax.all_gather(value, "blk", axis=axis, tiled=True, axis_index_groups=sets)


def own_share(value, repeat, axis):
    if repeat == 1:
        return value
    count = repeat // 2
    sets = [list(range(at, at + count)) for at in range(0, lax.axis_size("blk"), count)]
    value = lax.psum(value, "head")
    if count > 1:
        value = lax.psum(value, "blk", axis_index_groups=sets)
    size = value.shape[axis] // repeat
    at = jnp.mod(lax.axis_index("blk") * 2 + lax.axis_index("head"), repeat)
    return lax.dynamic_slice_in_dim(value, at * size, size, axis)


def body(tokens, w_qkv, w_out, w_ff1, w_ff2, norm_gains, norm_biases, proj_biases, ff_bias, doc_starts, d_out):
    blks = lax.axis_size("blk")
    repeat = blks * 2 // 32
    groups = blks // GROUP
    tok, dim = tokens.shape
    half_rows = 4 * tok
    total_rows = blks * 2 * tok
    blk = lax.axis_index("blk")
    joined = gather_repeat(jnp.concatenate([w_qkv, w_out, w_ff1], axis=1), repeat, 0)
    joined = jnp.pad(joined, ((0, -joined.shape[0] % 16), (0, 0)))
    shard_ff2 = gather_repeat(w_ff2, repeat, 0)
    small = pack_small(
        gather_repeat(norm_gains, repeat, 1), gather_repeat(norm_biases, repeat, 1),
        gather_repeat(proj_biases, repeat, 1), gather_repeat(ff_bias, repeat, 0),
    )
    bounds, query_ids, key_ids = doc_tables(
        doc_starts, lax.rem(blk, 2), lax.div(blk, GROUP), half_rows, total_rows
    )
    all3, all_ff2, params, ffb, queries, window = enter(repeat, groups, joined, shard_ff2, small, tokens)
    window = window.reshape(6 * half_rows, KW)
    context, sums = forward(bounds, queries, window, query_ids, key_ids)
    out, d_mid, grads, grad_o3, grad_ff2, sum_rows = middle(
        repeat, groups, context, tokens, d_out, params, ffb, all3, all_ff2
    )
    d_query, d_window = backward(bounds, queries, window, query_ids, key_ids, context, grads, sums)
    d_tokens, g_qkv, g_out, g_ff1, g_ff2, g_rows = leave(
        repeat, groups, d_query, d_window.reshape(3, 2 * half_rows, KW), tokens, d_mid, sum_rows, all3, grad_o3, grad_ff2
    )
    unit = lax.div(blk * 2 + lax.axis_index("head"), repeat)
    width = dim // 32
    rows = g_rows
    g_small = lax.dynamic_slice_in_dim(rows[:8], unit * width, width, 1)
    g_hidden = lax.dynamic_slice_in_dim(rows[8:].reshape(-1), unit * shard_ff2.shape[0], shard_ff2.shape[0], 0)
    g_small, g_hidden = own_share(g_small, repeat, 1), own_share(g_hidden, repeat, 0)
    return (
        out, d_tokens, own_share(g_qkv, repeat, 0), own_share(g_out, repeat, 0), own_share(g_ff1, repeat, 0),
        own_share(g_ff2, repeat, 0), g_small[0:2], g_small[2:4], g_small[4:8], g_hidden,
    )


def solution(mesh):
    rows, columns, flat = P(("blk", "head"), None), P(None, ("blk", "head")), P(("blk", "head"))
    return jax.shard_map(
        body,
        mesh=mesh,
        in_specs=(rows,) * 5 + (columns,) * 3 + (flat, P(), rows),
        out_specs=(rows,) * 6 + (columns,) * 3 + (flat,),
        check_vma=False,
    )
```

time: 1160 us -> 371 us (0.32); the launches traced: 1150 us -> 372 us
  waiting for transfers between devices: 373 us -> 0 us
  Pallas kernels: 0 us -> 347 us
  blocking collectives: 316 us -> 0 us
  starting transfers between devices: 163 us -> 0 us
  matrix products: 112 us -> 0 us
  other arithmetic: 74 us -> 7.19 us
  local copies, waits for them, and re-layouts: 66.1 us -> 17 us
  loops' own time: 22.6 us -> 0 us
  between operations: 18.8 us -> 0.72 us
    pallas_call x0 -> x5, Pallas kernels: none -> 347 us  [the longest x1 144 us: leave(): pl.pallas_call(functools.partial(leave_kernel, repeat, groups), out_shape...]
    reduce_scatter x3 -> x0, waiting for transfers between devices: 283 us -> none  [the longest x1 142 us: body(): lax.psum_scatter(grad_terms[3], ('blk', 'head'), scatter_dimension=0, til...]
    all_gather x3 -> x0, blocking collectives: 204 us -> none  [the longest x1 70.1 us: body(): lax.all_gather(proj_biases, ('blk', 'head'), axis=1, tiled=True)]
    ppermute x26 -> x0, starting transfers between devices: 152 us -> none  [from_behind(): return lax.ppermute(value, axis, pairs)]
    dot_general x46 -> x0, matrix products: 112 us -> none  [the longest x5 18 us: fold_block(): jnp.einsum('hqk,khd->qhd', exp_terms.astype(jnp.bfloat16), value_rows, pr...]
    unnamed x2 -> x0, blocking collectives: 97.3 us -> none
    unnamed x9 -> x0, waiting for transfers between devices: 59 us -> none
    reduce_sum x32 -> x2, other arithmetic: 31 us -> 2.16 us  [the longest x1 1.29 us: doc_tables(): live = jnp.sum((doc_starts < total_rows).astype(jnp.int32))]
  transfers between devices with their start and end apart: 37 -> 0, of which waited for: 12 -> 0; matrix products, arithmetic and copies ran while one was open for 20% -> 0% of each run, Pallas kernels for 0% -> 0%
where the time goes in v1:
time: 371 us; the launch traced here: 372 us
  Pallas kernels  347 us (94%)
  local copies, waits for them, and re-layouts  17 us (5%)
  other arithmetic  7.19 us (2%)
    pallas_call x1, Pallas kernels, leave(): pl.pallas_call(functools.partial(leave_kernel, repeat, groups), out_shape...  144 us
    pallas_call x1, Pallas kernels, enter(): pl.pallas_call(functools.partial(enter_kernel, repeat, groups), out_shape...  117 us
    pallas_call x1, Pallas kernels, middle(): pl.pallas_call(functools.partial(middle_kernel, repeat, groups), out_shap...  33.2 us
    pallas_call x1, Pallas kernels, backward(): pl.pallas_call(backward_kernel, out_shape=(shape(queries.shape, BF16), sh...  31.7 us
    pallas_call x1, Pallas kernels, forward(): pl.pallas_call(forward_kernel, out_shape=(shape((count, QW), F32), shape(...  20.5 us
    unnamed x8, local copies, waits for them, and re-layouts  9.06 us

profile of v1, /device:TPU:0, one launch (start us, length us, event | category | flops | bytes accessed | tf_op | source)
XLA Modules:
  0.0 372.1 jit_solution(7503654834241687761)
XLA Ops:
  0.7 1.3 fusion.14
  1.9 0.7 pad_bitcast_fusion
  2.6 0.1 pad.17.clone
  2.7 0.7 fusion.13
  3.4 0.7 maximum_maximum_fusion.small
  4.1 0.9 convert_reduce_fusion
  5.0 0.9 broadcast_remainder_fusion
  5.9 0.2 slice_reduce_fusion.1
  6.1 0.6 broadcast_in_dim.47.query_ids
  6.7 0.2 compare_reduce_fusion.1
  6.9 0.2 select_reduce_fusion
  7.1 0.6 pad_add_fusion.bounds
  7.7 1.8 fusion.4.shard3
  9.4 3.8 %broadcast_in_dim.48.key_ids = s32[6144,128]{1,0:T(8,128)} broadcast(s32[6144]{0:T(1024)S(1)} %broadcast_remainder_fusion), dimensions={0} | broadcast | bytes 3170304 | tf_op jit(solution)/shard_map/broadcast_in_dim | solution.py:720
  13.3 117.5 %shard_map.186 = (bf16[768,6144]{1,0:T(8,128)(2,1)}, bf16[3072,768]{1,0:T(8,128)(2,1)}, f32[16,768]{1,0:T(8,128)}, f32[8,3072]{1,0:T(8,128)}, bf16[1024,256]{1,0:T(8,128)(2,1)}, /*index=5*/bf16[3,2048,384]{2,1,0:T(8,128)(2,1)}) custom-call(bf16[32,6144]{1,0:T(8,128)(2,1)} %fusion.4.shard3, bf16[96,768]{1,0:T(8,128)(2,1)} %shard_ff2.1, ...), custom_call_target="tpu_custom_call" | custom-call | tf_op jit(solution)/shard_map/pallas_call | solution.py:511
  130.7 20.5 %shard_map.187 = (f32[1024,256]{1,0:T(8,128)}, f32[8,1024]{1,0:T(8,128)}) custom-call(s32[2,2]{1,0:T(2,128)} %pad_add_fusion.bounds, bf16[1024,256]{1,0:T(8,128)(2,1)} %get-tuple-element.32.queries, bf16[6144,384]{1,0:T(8,128)(2,1)} %bitcast.6, s32[8,1024]{1,0:T(8,128)} %broadcast_in_dim.47.query_ids, s32[6144,128]{1,0:T(8,128)} %broadcast_in_dim.48.key_ids), custom_call_target="tpu_custom_call" | custom-call | tf_op jit(solution)/shard_map/pallas_call | solution.py:615
  151.2 33.2 %shard_map.188 = (bf16[256,768]{1,0:T(8,128)(2,1)}, f32[256,768]{1,0:T(8,128)}, bf16[1024,256]{1,0:T(8,128)(2,1)}, bf16[768,3840]{1,0:T(8,128)(2,1)}, bf16[3072,768]{1,0:T(8,128)(2,1)}, /*index=5*/f32[16,768]{1,0:T(8,128)}) custom-call(f32[1024,256]{1,0:T(8,128)} %get-tuple-element.34.context, bf16[256,768]{1,0:T(8,128)(2,1)} %tokens.5, ...), custom_call_target="tpu_custom_call" | custom-call | tf_op jit(solution)/shard_map/pallas_call | solution.py:829
  184.4 31.7 %shard_map.189 = (bf16[1024,256]{1,0:T(8,128)(2,1)}, bf16[6144,384]{1,0:T(8,128)(2,1)}) custom-call(s32[2,2]{1,0:T(2,128)} %pad_add_fusion.bounds, bf16[1024,256]{1,0:T(8,128)(2,1)} %get-tuple-element.32.queries, bf16[6144,384]{1,0:T(8,128)(2,1)} %bitcast.7, s32[8,1024]{1,0:T(8,128)} %broadcast_in_dim.47.query_ids, s32[6144,128]{1,0:T(8,128)} %broadcast_in_dim.48.key_ids, ...), custom_call_target="tpu_custom_call" | custom-call | tf_op jit(solution)/shard_map/pallas_call | solution.py:688
  216.1 0.0 copy-start
  216.1 144.4 %shard_map.190 = (bf16[256,768]{1,0:T(8,128)(2,1)}, f32[24,2304]{1,0:T(8,128)}, f32[24,768]{1,0:T(8,128)}, f32[24,3072]{1,0:T(8,128)}, f32[96,768]{1,0:T(8,128)}, /*index=5*/f32[16,768]{1,0:T(8,128)}) custom-call(bf16[1024,256]{1,0:T(8,128)(2,1)} %get-tuple-element.42.d_query, bf16[3,2048,384]{2,1,0:T(8,128)(2,1)} %bitcast.8, bf16[256,768]{1,0:T(8,128)(2,1)} %tokens.5, ...), custom_call_target="tpu_custom_call" | custom-call | tf_op jit(solution)/shard_map/pallas_call | solution.py:1035
  360.5 0.8 fusion.15
  361.2 0.6 dynamic_slice.11
  361.8 0.1 constant_dynamic-slice_fusion
  361.9 0.6 slice.26
  362.5 0.6 fusion.16
  363.1 0.0 copy-done
  363.1 0.7 copy.27
  363.8 1.8 copy.28
  365.6 1.6 copy.29
  367.2 1.5 copy.30
  368.7 1.7 copy.31
  370.4 1.7 copy.32
  (7 shorter events, 0.1 us)
Async XLA Ops:
  216.1 147.0 %copy-start = (bf16[256,768]{1,0:T(8,128)(2,1)S(1)}, bf16[256,768]{1,0:T(8,128)(2,1)}, u32[]{:S(2)}) copy-start(bf16[256,768]{1,0:T(8,128)(2,1)} %get-tuple-element.74) | copy-start | bytes 1179652

commit v2 on v1

v2 whole, which is shorter than its diff:
```python
import functools

import jax
import jax.numpy as jnp
from jax import lax
from jax.experimental import pallas as pl
from jax.experimental.pallas import tpu as pltpu
from jax.sharding import PartitionSpec as P

H = 12
HD = 64
DOC_MOST = 2048
EPSILON = 1e-06
NEGATIVE = -1e30
MESH = pl.DeviceIdType.MESH
F32 = jnp.float32
BF16 = jnp.bfloat16
VMEM_BYTES = 60 * 1024 * 1024
CHIPS = 4
GROUP = 4
QW = 256
KW = 384
HW = (H // CHIPS) * HD
PW = QW + KW


def div(a, b):
    return lax.div(a, jnp.int32(b))


def rem(a, b):
    return lax.rem(a, jnp.int32(b))


def nn(a, b):
    return lax.dot_general(a, b, (((1,), (0,)), ((), ())), preferred_element_type=F32)


def nt(a, b):
    return lax.dot_general(a, b, (((1,), (1,)), ((), ())), preferred_element_type=F32)


def tn(a, b):
    return lax.dot_general(a, b, (((0,), (0,)), ((), ())), preferred_element_type=F32)


def rows_at(start, count, unit=16):
    return pl.ds(pl.multiple_of(start, unit), count)


class Place:
    def __init__(self, repeat, groups):
        self.repeat = repeat
        blk, head = lax.axis_index("blk"), lax.axis_index("head")
        self.index = blk * 2 + head
        self.unit = div(self.index, repeat)
        self.core, self.x, self.y = rem(blk, 2), rem(div(blk, 2), 2), head
        self.group, self.groups = div(blk, GROUP), groups
        self.bits = [rem(div(self.unit, 1 << k), 2) for k in range(5)]
        others = [self.index + (1 - 2 * self.bits[k]) * (repeat << k) for k in range(5)]
        self.partners = [{"blk": div(other, 2), "head": rem(other, 2)} for other in others]

    def bit(self, k):
        return self.bits[k]

    def partner(self, k):
        return self.partners[k]

    def member(self, x, core, y):
        return {"blk": self.group * GROUP + 2 * x + core, "head": y}

    def beside(self, step):
        group = rem(self.group + self.groups + step, self.groups)
        return {"blk": group * GROUP + 2 * self.x + self.core, "head": self.y}

    def greet(self, cube=True, group=True, beside=True):
        barrier = pltpu.get_barrier_semaphore()
        partners = []
        if cube:
            partners += [self.partner(k) for k in range(5)]
        if group:
            partners += [
                self.member(
                    rem(self.x + dx, 2), rem(self.core + dc, 2), rem(self.y + dy, 2)
                )
                for dx in range(2)
                for dc in range(2)
                for dy in range(2)
                if dx + dc + dy
            ]
        if beside:
            partners += [self.beside(1), self.beside(-1)]
        for partner in partners:
            pl.semaphore_signal(barrier, inc=1, device_id=partner, device_id_type=MESH)
        pl.semaphore_wait(barrier, len(partners))


def remote(src, dst, send, recv, device):
    return pltpu.make_async_remote_copy(
        src_ref=src, dst_ref=dst, send_sem=send, recv_sem=recv, device_id=device, device_id_type=MESH
    )


class Pieces:
    def __init__(self, place, ref, rows, first, width, order, by_columns):
        self.place, self.ref, self.rows, self.first, self.width = place, ref, rows, first, width
        self.order, self.by_columns = order, by_columns
        if by_columns is not None:
            self.shape = (rows, width // 2) if by_columns else (rows // 2, width)
        self.deltas = [(1 - 2 * place.bit(k)) * (1 << k) for k in order]
        self.units = {0: place.unit}
        self.own = self.piece(0)

    def unit_of(self, mask):
        if mask not in self.units:
            at = mask.bit_length() - 1
            self.units[mask] = self.unit_of(mask - (1 << at)) + self.deltas[at]
        return self.units[mask]

    def region(self, unit):
        slab, half = div(unit, 2), rem(unit, 2)
        if self.by_columns:
            return (
                rows_at(slab * self.rows, self.rows),
                rows_at(self.first + half * self.shape[1], self.shape[1], 128),
            )
        return (rows_at(unit * self.shape[0], self.shape[0]), pl.ds(self.first, self.width))

    def piece(self, mask):
        return self.ref.at[self.region(self.unit_of(mask))]


class Gather(Pieces):
    def begin(self, send, recv, until=5):
        self.send, self.recv = send, recv
        self.feed(0, 0, until)

    def copy(self, phase, mask, ref):
        at = (1 << phase) - 1 + mask
        return remote(ref, ref, self.send.at[at], self.recv.at[at], self.place.partner(self.order[phase]))

    def feed(self, mask, phase, until=5):
        if phase < until:
            ref = self.piece(mask)
            for later in range(phase, until):
                self.copy(later, mask, ref).start()

    def release(self, phase):
        for mask in range(1 << phase):
            self.feed(mask, phase)

    def step(self, phase, until=5):
        for mask in range(1 << phase):
            self.copy(phase, mask, self.own).wait_recv()
            self.feed(mask + (1 << phase), phase + 1, until)

    def finish(self):
        for phase in range(5):
            for mask in range(1 << phase):
                self.copy(phase, mask, self.own).wait_send()


class Scatter(Pieces):
    def begin(self, landing, send, recv):
        self.landing, self.send, self.recv = landing, send, recv
        for j in range(16):
            self.give(0, j)

    def slot(self, phase, j):
        return 32 - (1 << (5 - phase)) + j

    def copy(self, phase, j, ref):
        at = self.slot(phase, j)
        return remote(
            ref, self.landing.at[at], self.send.at[at], self.recv.at[at], self.place.partner(self.order[phase])
        )

    def give(self, phase, j):
        self.copy(phase, j, self.piece((2 * j + 1) * (1 << phase))).start()

    def absorb(self, phase, j):
        self.copy(phase, j, self.own).wait_recv()
        rows, columns = self.region(self.unit_of(j * (2 << phase)))
        total = self.ref[rows, columns].astype(F32) + self.landing[self.slot(phase, j)].astype(F32)
        self.ref[rows, columns] = total.astype(BF16)
        return total

    def step(self, phase):
        half = 1 << (3 - phase)
        for jj in range(half):
            self.absorb(phase, 2 * jj + 1)
            self.give(phase + 1, jj)
        for jj in range(half):
            self.absorb(phase, 2 * jj)

    def last(self):
        return self.absorb(4, 0)

    def finish(self):
        for phase in range(5):
            for j in range(1 << (4 - phase)):
                self.copy(phase, j, self.own).wait_send()


class GatherBlocks(Gather):
    def __init__(self, place, ref, order):
        self.shape = ref.shape[1:]
        Pieces.__init__(self, place, ref, 0, 0, 0, order, None)

    def piece(self, mask):
        return self.ref.at[self.unit_of(mask)]


class ScatterBlocks(Scatter):
    def __init__(self, place, ref, order, until):
        Pieces.__init__(self, place, ref, 0, 0, 0, order, None)
        self.until = until

    def piece(self, mask):
        return self.ref.at[self.unit_of(mask)]

    def give(self, phase, j):
        if phase < self.until:
            Scatter.give(self, phase, j)

    def absorb(self, phase, j):
        self.copy(phase, j, self.own).wait_recv()
        unit = self.unit_of(j * (2 << phase))
        total = self.ref[unit].astype(F32) + self.landing[self.slot(phase, j)].astype(F32)
        self.ref[unit] = total.astype(BF16)
        return total

    def finish(self):
        for phase in range(self.until):
            for j in range(1 << (4 - phase)):
                self.copy(phase, j, self.own).wait_send()


def to_heads(place, packed, landed, send, recv, part=None):
    tok = packed.shape[1] if part is None else part.shape[0]
    mine = rows_at(2 * tok * place.core + tok * place.y, tok)
    slot = 2 * place.core + place.y
    alone = place.core == place.x
    for dx, dy in ((0, 0), (1, 0), (0, 1), (1, 1)):
        if True:
            tx, ty = rem(place.x + dx, 2), rem(place.y + dy, 2)
            copy = remote(
                packed.at[2 * tx + ty] if part is None else part,
                landed.at[mine],
                send.at[2 * dx + dy],
                recv.at[slot],
                place.member(tx, place.x, ty),
            )
            if dx + dy:
                copy.start()
            else:
                pl.when(jnp.logical_not(alone))(copy.start)

                @pl.when(alone)
                def _(tx=tx, ty=ty):
                    landed[mine] = packed[2 * tx + ty] if part is None else part[...]


def to_heads_wait_one(place, landed, send, recv, cs, ys):
    tok = landed.shape[0] // 4
    part = landed.at[pl.ds(0, tok)]
    copy = remote(part, part, send.at[0], recv.at[2 * cs + ys], place.member(place.x, 1 - place.core, place.y))
    own = (place.core == place.x) & (place.core == cs) & (place.y == ys)
    pl.when(jnp.logical_not(own))(copy.wait_recv)


def to_heads_wait(place, landed, send, recv):
    for cs in range(2):
        for ys in range(2):
            to_heads_wait_one(place, landed, send, recv, cs, ys)


def to_heads_drain(place, landed, send, recv):
    part = landed.at[pl.ds(0, landed.shape[0] // 4)]
    for at in range(4):
        copy = remote(part, part, send.at[at], recv.at[0], place.member(place.x, 1 - place.core, place.y))
        if at:
            copy.wait_send()
        else:
            pl.when(place.core != place.x)(copy.wait_send)


def to_tokens(place, rows, landed, send, recv):
    tok = landed.shape[1]
    chip = 2 * place.x + place.y
    for cs in range(2):
        for ys in range(2):
            part = pl.ds(2 * tok * cs + tok * ys, tok)
            own = (place.core == place.x) & (place.core == cs) & (place.y == ys)
            copy = remote(
                rows.at[part], landed.at[chip], send.at[2 * cs + ys], recv.at[chip], place.member(place.core, cs, ys)
            )
            pl.when(jnp.logical_not(own))(copy.start)

            @pl.when(own)
            def _(part=part):
                landed[chip] = rows[part]


def to_tokens_wait(place, rows, landed, send, recv):
    for xs in range(2):
        for ys in range(2):
            at = 2 * xs + ys
            own = (place.core == place.x) & (place.x == xs) & (place.y == ys)
            copy = remote(
                landed.at[at], landed.at[at], send.at[at], recv.at[at], place.member(place.x, 1 - place.core, place.y)
            )
            pl.when(jnp.logical_not(own))(copy.wait_recv)


def to_tokens_drain(place, rows, landed, send, recv):
    for cs in range(2):
        for ys in range(2):
            own = (place.core == place.x) & (place.core == cs) & (place.y == ys)
            at = 2 * cs + ys
            copy = remote(
                landed.at[at], landed.at[at], send.at[at], recv.at[at], place.member(place.x, 1 - place.core, place.y)
            )
            pl.when(jnp.logical_not(own))(copy.wait_send)


def spread_rows(small, per, width, rows):
    lane = lax.broadcasted_iota(jnp.int32, (128, width), 1).astype(F32)
    spot = lane - per * jnp.floor((lane + 0.5) * (1.0 / per))
    pick = (spot == lax.broadcasted_iota(jnp.int32, (128, width), 0).astype(F32)).astype(BF16)
    wide = nn(small.astype(BF16), pick).reshape(32, rows, width)
    low = lax.broadcasted_iota(jnp.int32, wide.shape, 0) * per
    column = lax.broadcasted_iota(jnp.int32, wide.shape, 2)
    return jnp.sum(jnp.where((column >= low) & (column < low + per), wide, 0.0), axis=0)


AG_PLAN = dict(out=(4, 3, 0, 2, 1), ff1=(4, 3, 0, 2, 1), ff2=(4, 3, 2, 0, 1))
AG_HEADS = (2, 0, 4, 3, 1)
RS_PLAN = dict(out=(1, 2, 0, 3, 4), ff1=(1, 2, 0, 3, 4), ff2=(1, 0, 2, 3, 4))
RS_HEADS = (1, 3, 4, 2, 0)
REST = ("ff2", "ff1", "out")


def matrices(dim, ff):
    return (("out", 0, dim), ("ff1", dim, ff))


def plane(place, dx, dy):
    tx, ty = rem(place.x + dx, 2), rem(place.y + dy, 2)
    return 2 * tx + ty, place.member(tx, place.core, ty)


def enter_kernel(
    repeat, groups,
    shard_qkv, shard2, shard_ff2, small, tokens,
    all2_out, ff2_out, params_out, ffb_out, q_out, kv_out, rows_out, heads_out,
    stage, all2, all_ff2, q_rows, window, rows, pack_w, blocks, heads,
    y_sems, gather_send, gather_recv, block_send, block_recv, plane_send, plane_recv,
    row_send, row_recv, near_send, near_recv, side_send, side_recv, local,
):
    place = Place(repeat, groups)
    dim = all2.shape[0]
    ff = all_ff2.shape[0]
    tok = tokens.shape[0]
    unit_rows = dim // 32
    slab = 2 * unit_rows
    half = 4 * tok
    own_ff2 = pltpu.make_async_copy(
        shard_ff2, all_ff2.at[rows_at(place.unit * (ff // 32), ff // 32)], local.at[0]
    )
    own_ff2.start()
    wide = shard_qkv[...].astype(F32)
    for chip in range(CHIPS):
        cut = [wide[:, part * dim + HW * chip:part * dim + HW * (chip + 1)] for part in range(3)]
        block = jnp.concatenate([cut[0], jnp.zeros((unit_rows, QW - HW), F32), cut[1], cut[2]], axis=1)
        pack_w[chip] = jnp.concatenate([block, small[...].astype(F32)], axis=0).astype(BF16)
    role = 2 * place.x + place.y
    blocks[place.unit] = pack_w[role]
    place.greet()
    plane_copies = []
    if repeat == 1:
        for dx, dy in ((1, 1), (1, 0), (0, 1)):
            chip, device = plane(place, dx, dy)
            at = 2 * dx + dy
            copy = remote(pack_w.at[chip], blocks.at[place.unit], plane_send.at[at], plane_recv.at[at], device)
            copy.start()
            plane_copies.append(copy)
    to_heads(place, None, rows, row_send, row_recv, tokens)
    cuts = matrices(dim, ff)
    y_copies = []

    def half_columns(at, which):
        name, first, width = cuts[at]
        return (slice(None), rows_at(first + which * (width // 2), width // 2, 128))

    for at in range(2):
        mine, other = half_columns(at, place.bit(0)), half_columns(at, 1 - place.bit(0))
        out = remote(shard2.at[other], stage.at[other], y_sems.at[at], y_sems.at[2 + at], place.partner(0))
        back = remote(shard2.at[mine], stage.at[mine], y_sems.at[at], y_sems.at[2 + at], place.partner(0))
        out.start()
        y_copies.append((out, back))

    by_heads = GatherBlocks(place, blocks, AG_HEADS)
    gathers = {name: Gather(place, all2, slab, first, width, AG_PLAN[name], True) for name, first, width in cuts}
    gathers["ff2"] = Gather(place, all_ff2, ff // 16, 0, dim, AG_PLAN["ff2"], False)
    here = rows_at(div(place.unit, 2) * slab, slab)

    def merge(at):
        y_copies[at][1].wait_recv()
        name, first, width = cuts[at]
        low = place.bit(0) == 0
        for column in range(0, width // 2, 256):
            size = min(256, width // 2 - column)
            part = rows_at(first + place.bit(0) * (width // 2) + column, size, 128)
            mine, other = shard2[:unit_rows, part].astype(F32), stage[:unit_rows, part].astype(F32)
            whole = jnp.concatenate([jnp.where(low, mine, other), jnp.where(low, other, mine)], axis=0)
            all2[here, part] = whole.astype(BF16)
        gathers[name].begin(gather_send.at[at], gather_recv.at[at])

    by_heads.send, by_heads.recv = block_send, block_recv
    if repeat == 1:
        for copy in plane_copies:
            copy.wait_recv()
        by_heads.release(2)
    else:
        by_heads.feed(0, 0)
        by_heads.step(0)
        by_heads.step(1)
    own_ff2.wait()
    by_heads.step(2)
    gathers["ff2"].begin(gather_send.at[2], gather_recv.at[2])
    merge(1)
    merge(0)
    by_heads.step(3)
    for name in REST:
        gathers[name].step(0)
    by_heads.step(4)

    def compact(pair, carry):
        whole = jnp.concatenate(
            [blocks[2 * pair][:unit_rows].astype(F32), blocks[2 * pair + 1][:unit_rows].astype(F32)], axis=0
        )
        heads[rows_at(pair * slab, slab)] = whole.astype(BF16)
        return carry

    lax.fori_loop(0, 16, compact, 0)
    params_out[...] = spread_rows(blocks[:, unit_rows:, 0:128].astype(F32).reshape(-1, 128), unit_rows, dim, 8)
    bias = jnp.zeros((2, PW), F32)
    for chip in range(CHIPS):
        cut = params_out[4:6, HW * chip:HW * (chip + 1)]
        query = jnp.concatenate([cut[0:1], jnp.zeros((1, PW - HW), F32)], axis=1)
        value = jnp.concatenate([jnp.zeros((1, PW - HW), F32), cut[1:2]], axis=1)
        bias = jnp.where(role == chip, query + value, bias)
    sibling = place.member(place.x, 1 - place.core, place.y)

    def stretch(slot, core):
        return window.at[slot].at[rows_at(half * core, half)]

    def part_of(slot, at):
        return window.at[slot].at[rows_at(half * place.core + tok * at, tok)]

    def side(to, at):
        return remote(
            part_of(1, at), part_of(2 * to, at), side_send.at[to, at], side_recv.at[to, at], place.beside(1 - 2 * to)
        )

    def near(at):
        ref = stretch(1, place.core) if at == 0 else stretch(2 - 2 * place.core, place.core)
        return remote(ref, ref, near_send.at[at], near_recv.at[at], sibling)

    for ys in (place.y, 1 - place.y):
        for cs in range(2):
            to_heads_wait_one(place, rows, row_send, row_recv, cs, ys)
            at = 2 * cs + ys
            part = rows_at(at * tok, tok)
            made = nn(rows[part, :], heads[...]) + bias[0:1]
            window[1, rows_at(half * place.core + at * tok, tok)] = made[:, QW:].astype(BF16)
            side(0, at).start()
            side(1, at).start()
            q_rows[part, :] = made[:, :QW].astype(BF16)
    near(0).start()
    hidden = blocks[:, unit_rows:, 128:256].astype(F32).reshape(-1, 128)
    ffb_out[...] = spread_rows(hidden, ff // 32, ff, 8)
    for name in REST:
        gathers[name].step(1)
    first_copies = [
        pltpu.make_async_copy(q_rows, q_out, local.at[2]),
        pltpu.make_async_copy(rows, rows_out, local.at[3]),
        pltpu.make_async_copy(heads, heads_out, local.at[4]),
    ]
    for copy in first_copies:
        copy.start()
    for phase in range(2, 5):
        for name in REST:
            gathers[name].step(phase)
    for gather in gathers.values():
        gather.finish()
    copies = [
        pltpu.make_async_copy(all2, all2_out, local.at[0]),
        pltpu.make_async_copy(all_ff2, ff2_out, local.at[1]),
    ]
    for copy in copies:
        copy.start()
    for at in range(4):
        side(0, at).wait_recv()
        side(1, at).wait_recv()
    near(1).start()
    near(0).wait_recv()
    near(1).wait_recv()
    last = pltpu.make_async_copy(window, kv_out, local.at[5])
    last.start()
    for at in range(2):
        y_copies[at][0].wait_send()
        near(at).wait_send()
        for part in range(4):
            side(at, part).wait_send()
    for copy in plane_copies:
        copy.wait_send()
    for phase in range(2 if repeat == 1 else 0, 5):
        for mask in range(1 << phase):
            by_heads.copy(phase, mask, by_heads.own).wait_send()
    to_heads_drain(place, rows, row_send, row_recv)
    for copy in first_copies + copies + [last]:
        copy.wait()


VM = pl.BlockSpec(memory_space=pltpu.VMEM)
HBM = pl.BlockSpec(memory_space=pl.ANY)
SM = pl.BlockSpec(memory_space=pltpu.SMEM)
DMA = pltpu.SemaphoreType.DMA


def enter(repeat, groups, shard_qkv, shard2, shard_ff2, small, tokens):
    tok, dim = tokens.shape
    joined = shard2.shape[1]
    ff = shard_ff2.shape[0] * 32
    shape = jax.ShapeDtypeStruct
    vm = pltpu.VMEM
    return pl.pallas_call(
        functools.partial(enter_kernel, repeat, groups),
        out_shape=(
            shape((dim, joined), BF16), shape((ff, dim), BF16), shape((8, dim), F32), shape((8, ff), F32),
            shape((4 * tok, QW), BF16), shape((3, 8 * tok, KW), BF16), shape((4 * tok, dim), BF16),
            shape((dim, PW), BF16),
        ),
        in_specs=[VM] * 5,
        out_specs=(HBM, HBM, VM, VM, HBM, HBM, HBM, HBM),
        scratch_shapes=[
            vm(shard2.shape, BF16), vm((dim, joined), BF16), vm((ff, dim), BF16),
            vm((4 * tok, QW), BF16), vm((3, 8 * tok, KW), BF16), vm((4 * tok, dim), BF16),
            vm((CHIPS, shard2.shape[0], PW), BF16), vm((32, shard2.shape[0], PW), BF16), vm((dim, PW), BF16),
            DMA((4,)), DMA((3, 31)), DMA((3, 31)), DMA((31,)), DMA((31,)), DMA((4,)), DMA((4,)),
            DMA((4,)), DMA((4,)), DMA((2,)), DMA((2,)), DMA((2, 4)), DMA((2, 4)), DMA((6,)),
        ],
        compiler_params=pltpu.CompilerParams(
            collective_id=1, has_side_effects=True, vmem_limit_bytes=VMEM_BYTES
        ),
    )(shard_qkv, shard2, shard_ff2, small, tokens)


def pack_small(norm_gains, norm_biases, proj_biases, ff_bias):
    rows = jnp.concatenate([norm_gains, norm_biases, proj_biases], axis=0)
    rows = jnp.pad(rows, ((0, 0), (0, 128 - rows.shape[1])))
    hidden = jnp.pad(ff_bias[None], ((0, 7), (0, PW - 128 - ff_bias.shape[0])))
    return jnp.concatenate([rows, hidden], axis=1)


QT = 512
KT = 512


def lane_mask(shape, low, high, axis):
    lane = lax.broadcasted_iota(jnp.int32, shape, axis)
    return (lane >= low) & (lane < high)


HEAD_QUERY = ((0, 0), (0, 64), (128, 0))
HEAD_VALUE = ((128, 64), (256, 0), (256, 64))
HEAD_CONTEXT = ((0, 64), (128, 0), (128, 64))


def head_rows(ref, rows, spot):
    tile, place = spot
    part = ref[rows, tile:tile + 128]
    return jnp.where(lane_mask(part.shape, place, place + HD, 1), part, jnp.zeros_like(part))


def doc_spans(starts, spans, total_rows):
    half = spans.shape[1]
    blk = lax.axis_index("blk")
    origin = (div(blk, GROUP) - 1) * 2 * half
    first = origin + (2 + rem(blk, 2)) * half
    far = jnp.int32(1 << 30)
    shape = (half // 128, 128)
    places = first + 128 * lax.broadcasted_iota(jnp.int32, shape, 0) + lax.broadcasted_iota(jnp.int32, shape, 1)
    edges = range(0, half, QT)

    def one(at, state):
        low, high, last, lows, highs = state
        start = starts[at]
        live = start < total_rows
        below = jnp.where(live, start, -far)
        above = jnp.where(live, start, far)
        low = jnp.where(below <= places, jnp.maximum(low, below), low)
        high = jnp.where(above > places, jnp.minimum(high, above), high)
        lows = tuple(jnp.where(below <= first + edge, jnp.maximum(old, below), old) for edge, old in zip(edges, lows))
        highs = tuple(
            jnp.where(above > first + edge + QT - 1, jnp.minimum(old, above), old) for edge, old in zip(edges, highs)
        )
        return low, high, jnp.maximum(last, below), lows, highs

    low, high, last, lows, highs = lax.fori_loop(
        0, starts.shape[0], one,
        (
            jnp.full(shape, -far), jnp.full(shape, far), -far,
            tuple(-far for _ in edges), tuple(far for _ in edges),
        ),
    )
    start, end = last - total_rows, starts[0] + total_rows
    low = jnp.where(low == -far, start, low) - origin
    high = jnp.where(high == far, end, high) - origin
    for at in range(shape[0]):
        spans[0:1, at * 128:(at + 1) * 128] = low[at:at + 1]
        spans[1:2, at * 128:(at + 1) * 128] = high[at:at + 1]
    tiles = []
    for old_low, old_high in zip(lows, highs):
        begin = jnp.where(old_low == -far, start, old_low) - origin
        finish = jnp.where(old_high == far, end, old_high) - origin
        tiles.append((div(begin, KT), div(finish + (KT - 1), KT)))
    return tiles


def meets(spans, columns, j):
    key = j * KT + lax.broadcasted_iota(jnp.int32, (KT, QT), 0)
    inside = (key >= spans[0:1, columns]) & (key < spans[1:2, columns])
    return jnp.where(inside, 0.0, NEGATIVE)


def forward_kernel(total_rows, starts, queries, window, context_out, sums_out, spans):
    count = queries.shape[0]
    scale = HD ** (-0.5)
    tiles = doc_spans(starts, spans, total_rows)

    for at, (begin, finish) in enumerate(tiles):
        rows = slice(at * QT, (at + 1) * QT)
        columns = rows
        scaled = [head_rows(queries, rows, HEAD_QUERY[head]) * jnp.asarray(scale, BF16) for head in range(3)]

        def visit(j, state, columns=columns, scaled=scaled):
            keys = rows_at(j * KT, KT)
            bias = meets(spans, columns, j)
            tops, terms, fresh = [], [], []
            scores = [
                nt(window[keys, tile_at:tile_at + 128], scaled[head]) + bias
                for head, (tile_at, place) in enumerate(HEAD_QUERY)
            ]
            for head in range(3):
                tops.append(jnp.maximum(state[3 * head], jnp.max(scores[head], axis=0, keepdims=True)))
            for head in range(3):
                terms.append(jnp.exp(scores[head] - tops[head]))
            for head in range(3):
                highest, total, weighted = state[3 * head:3 * head + 3]
                tile_at = HEAD_VALUE[head][0]
                factor = jnp.exp(highest - tops[head])
                total = total * factor + jnp.sum(terms[head], axis=0, keepdims=True)
                weighted = weighted * factor + tn(window[keys, tile_at:tile_at + 128], terms[head].astype(BF16))
                fresh += [tops[head], total, weighted]
            return tuple(fresh)

        start = []
        for head in range(3):
            start += [jnp.full((1, QT), NEGATIVE, F32), jnp.zeros((1, QT), F32), jnp.zeros((128, QT), F32)]
        state = lax.fori_loop(begin, finish, visit, tuple(start))
        made = []
        for head in range(3):
            highest, total, weighted = state[3 * head:3 * head + 3]
            whole = weighted / total
            place = HEAD_CONTEXT[head][1]
            made.append(jnp.where(lane_mask(whole.shape, place, place + HD, 0), whole, 0.0))
            sums_out[head:head + 1, columns] = highest + jnp.log(total)
        context_out[rows, 0:128] = made[0].T
        context_out[rows, 128:256] = (made[1] + made[2]).T


def forward(total_rows, starts, queries, window):
    count = queries.shape[0]
    shape = jax.ShapeDtypeStruct
    return pl.pallas_call(
        functools.partial(forward_kernel, total_rows),
        out_shape=(shape((count, QW), F32), shape((8, count), F32)),
        in_specs=[SM] + [VM] * 2,
        out_specs=(VM, VM),
        scratch_shapes=[pltpu.VMEM((8, count), jnp.int32)],
        compiler_params=pltpu.CompilerParams(vmem_limit_bytes=VMEM_BYTES),
    )(starts, queries, window)


def backward_kernel(total_rows, starts, queries, window, context, grads, sums, query_out, window_out, acc, spans):
    count = queries.shape[0]
    scale = HD ** (-0.5)
    acc[...] = jnp.zeros_like(acc)
    tiles = doc_spans(starts, spans, total_rows)

    for at, (begin, finish) in enumerate(tiles):
        rows = slice(at * QT, (at + 1) * QT)
        columns = rows
        scaled, grad, delta, sum_rows = [], [], [], []
        for head in range(3):
            scaled.append(head_rows(queries, rows, HEAD_QUERY[head]) * jnp.asarray(scale, BF16))
            mine = head_rows(grads, rows, HEAD_CONTEXT[head])
            tile_at = HEAD_CONTEXT[head][0]
            product = mine.astype(F32) * context[rows, tile_at:tile_at + 128]
            grad.append(mine)
            delta.append(
                lax.dot_general(
                    jnp.ones((8, 128), F32), product, (((1,), (1,)), ((), ())),
                    precision=lax.Precision.HIGHEST, preferred_element_type=F32,
                )[0:1]
            )
            sum_rows.append(sums[head:head + 1, columns])

        def visit(j, state, columns=columns, scaled=scaled, grad=grad, delta=delta, sum_rows=sum_rows):
            keys = rows_at(j * KT, KT)
            bias = meets(spans, columns, j)
            fresh, key_grads, value_grads = [], [], []
            for head in range(3):
                key = window[keys, HEAD_QUERY[head][0]:HEAD_QUERY[head][0] + 128]
                value = window[keys, HEAD_VALUE[head][0]:HEAD_VALUE[head][0] + 128]
                probs = jnp.exp((nt(key, scaled[head]) + bias) - sum_rows[head])
                spread = nt(value, grad[head])
                steps = (probs * (spread - delta[head])).astype(BF16)
                value_grads.append(nn(probs.astype(BF16), grad[head]))
                key_grads.append(nn(steps, scaled[head]))
                fresh.append(state[head] + tn(key, steps))
            acc[keys, 0:128] += key_grads[0] + key_grads[1]
            acc[keys, 128:256] += key_grads[2] + value_grads[0]
            acc[keys, 256:384] += value_grads[1] + value_grads[2]
            return tuple(fresh)

        state = lax.fori_loop(
            begin, finish, visit, tuple(jnp.zeros((128, QT), F32) for _ in range(3))
        )
        made = []
        for head in range(3):
            place = HEAD_QUERY[head][1]
            made.append(jnp.where(lane_mask(state[head].shape, place, place + HD, 0), state[head] * scale, 0.0))
        query_out[rows, 0:128] = (made[0] + made[1]).T.astype(BF16)
        query_out[rows, 128:256] = made[2].T.astype(BF16)

    def store(at, carry):
        rows = rows_at(at * KT, KT)
        window_out[rows, :] = acc[rows, :].astype(BF16)
        return carry

    lax.fori_loop(0, acc.shape[0] // KT, store, 0)


def backward(total_rows, starts, queries, window, context, grads, sums):
    shape = jax.ShapeDtypeStruct
    return pl.pallas_call(
        functools.partial(backward_kernel, total_rows),
        out_shape=(shape(queries.shape, BF16), shape(window.shape, BF16)),
        in_specs=[SM] + [VM] * 5,
        out_specs=(VM, VM),
        scratch_shapes=[pltpu.VMEM(window.shape, F32), pltpu.VMEM((8, queries.shape[0]), jnp.int32)],
        compiler_params=pltpu.CompilerParams(vmem_limit_bytes=VMEM_BYTES),
    )(starts, queries, window, context, grads, sums)


def norm_forward(values):
    center = values - jnp.mean(values, axis=-1, keepdims=True)
    scale = lax.rsqrt(jnp.mean(center * center, axis=-1, keepdims=True) + EPSILON)
    return center * scale, scale


def norm_backward(grad, unit_rows, scale, gain):
    inner = grad * gain
    gain_row = jnp.sum(grad * unit_rows, axis=0, keepdims=True)
    shift_row = jnp.sum(grad, axis=0, keepdims=True)
    back = scale * (
        inner
        - jnp.mean(inner, axis=-1, keepdims=True)
        - unit_rows * jnp.mean(inner * unit_rows, axis=-1, keepdims=True)
    )
    return back, gain_row, shift_row


def column_sum(values):
    return jnp.sum(values.astype(F32), axis=0, keepdims=True)


def middle_kernel(
    repeat, groups,
    context, tokens, d_out, params, ffb, all2, all_ff2,
    out, d_mid_out, grads_out, grad_o3, grad_ff2, sum_rows,
    w_out, w_ff1, w_ff2, ctx_rows, parts, pack, grad_rows, act, slope, d_pre,
    send, recv, back_send, back_recv, local,
):
    place = Place(repeat, groups)
    tok, dim = tokens.shape
    ff = w_ff1.shape[1]
    loads = [
        pltpu.make_async_copy(all2.at[:, pl.ds(0, dim)], w_out, local.at[0]),
        pltpu.make_async_copy(all2.at[:, pl.ds(dim, ff)], w_ff1, local.at[1]),
        pltpu.make_async_copy(all_ff2, w_ff2, local.at[2]),
    ]
    for load in loads:
        load.start()
    ctx_rows[...] = context[...].astype(BF16)
    place.greet(cube=False, beside=False)
    to_tokens(place, ctx_rows, parts, send, recv)
    to_tokens_wait(place, ctx_rows, parts, send, recv)
    joined = jnp.concatenate([parts[chip][:, QW - HW:].astype(F32) for chip in range(CHIPS)], axis=1).astype(BF16)
    loads[0].wait()
    gains, shifts = [params[at:at + 1, :] for at in (0, 1)], [params[at:at + 1, :] for at in (2, 3)]
    mid = tokens[...].astype(F32) + (nn(joined, w_out[...]) + params[6:7, :])
    unit_first, scale_first = norm_forward(mid)
    hidden = unit_first * gains[0] + shifts[0]
    low = hidden.astype(BF16)
    loads[1].wait()
    loads[2].wait()
    ff_out = jnp.zeros((tok, dim), F32)
    for first in range(0, ff, dim):
        cut = slice(first, first + dim)
        pre = nn(low, w_ff1[:, cut]) + ffb[0:1, cut]
        bell = 0.5 * (1.0 + lax.erf(pre * 0.7071067811865476))
        made = (pre * bell).astype(BF16)
        act[:, cut] = made
        slope[:, cut] = bell + pre * jnp.exp(-0.5 * pre * pre) * 0.3989422804014327
        ff_out = ff_out + nn(made, w_ff2[cut, :])
    unit_second, scale_second = norm_forward(hidden + (ff_out + params[7:8, :]))
    out[...] = (unit_second * gains[1] + shifts[1]).astype(BF16)
    d_sum, gain_second, shift_second = norm_backward(d_out[...].astype(F32), unit_second, scale_second, gains[1])
    d_ff = d_sum.astype(BF16)
    d_hidden = d_sum
    for first in range(0, ff, dim):
        cut = slice(first, first + dim)
        made = (nt(d_ff, w_ff2[cut, :]) * slope[:, cut]).astype(BF16)
        d_pre[:, cut] = made
        d_hidden = d_hidden + nt(made, w_ff1[:, cut])
    d_mid, gain_first, shift_first = norm_backward(d_hidden, unit_first, scale_first, gains[0])
    d_mid_out[...] = d_mid
    d_attn = d_mid.astype(BF16)
    d_context = nt(d_attn, w_out[...])
    for chip in range(CHIPS):
        pack[chip] = jnp.concatenate(
            [jnp.zeros((tok, QW - HW), F32), d_context[:, HW * chip:HW * (chip + 1)]], axis=1
        ).astype(BF16)
    to_heads(place, pack, grad_rows, back_send, back_recv)
    for first in range(0, ff, dim):
        cut = slice(first, first + dim)
        grad_ff2[cut, :] = tn(act[:, cut], d_ff).astype(BF16)
        grad_o3[:, dim + first:2 * dim + first] = tn(low, d_pre[:, cut]).astype(BF16)
        sum_rows[8 + first // dim:9 + first // dim, :] = column_sum(d_pre[:, cut])
    grad_o3[:, 0:dim] = tn(joined, d_attn).astype(BF16)
    for at, row in enumerate(
        (
            gain_first, gain_second, shift_first, shift_second,
            jnp.zeros((1, dim), F32), jnp.zeros((1, dim), F32), column_sum(d_attn), column_sum(d_ff),
        )
    ):
        sum_rows[at:at + 1, :] = row
    sum_rows[8 + ff // dim:, :] = jnp.zeros((8 - ff // dim, dim), F32)
    to_heads_wait(place, grad_rows, back_send, back_recv)
    grads_out[...] = grad_rows[...]
    to_tokens_drain(place, ctx_rows, parts, send, recv)
    to_heads_drain(place, grad_rows, back_send, back_recv)


def middle(repeat, groups, context, tokens, d_out, params, ffb, all2, all_ff2):
    tok, dim = tokens.shape
    ff = all_ff2.shape[0]
    shape = jax.ShapeDtypeStruct
    vm = pltpu.VMEM
    return pl.pallas_call(
        functools.partial(middle_kernel, repeat, groups),
        out_shape=(
            shape((tok, dim), BF16), shape((tok, dim), F32), shape((4 * tok, QW), BF16),
            shape((dim, dim + ff), BF16), shape((ff, dim), BF16), shape((16, dim), F32),
        ),
        in_specs=[VM] * 5 + [HBM] * 2,
        out_specs=(VM,) * 6,
        scratch_shapes=[
            vm((dim, dim), BF16), vm((dim, ff), BF16), vm((ff, dim), BF16), vm((4 * tok, QW), BF16),
            vm((CHIPS, tok, QW), BF16), vm((CHIPS, tok, QW), BF16), vm((4 * tok, QW), BF16),
            vm((tok, ff), BF16), vm((tok, ff), F32), vm((tok, ff), BF16),
            DMA((4,)), DMA((4,)), DMA((4,)), DMA((4,)), DMA((4,)),
        ],
        compiler_params=pltpu.CompilerParams(collective_id=2, has_side_effects=True, vmem_limit_bytes=VMEM_BYTES),
    )(context, tokens, d_out, params, ffb, all2, all_ff2)


def leave_kernel(
    repeat, groups,
    d_query, d_window, rows, heads, d_mid, sum_rows, grad_o2, grad_ff2_in,
    d_tokens, g_qkv, g_out, g_ff1, g_ff2, g_rows,
    grad2, grad_ff2, land_out, land_ff1, land_ff2, blocks, land_blocks, role_land,
    near_land, side_land, joint, joined, partial, parts, swap_out, swap_in, rows_mine, rows_land,
    grad_send, grad_recv, block_send, block_recv, plane_send, plane_recv, near_send, near_recv, side_send, side_recv,
    part_send, part_recv, swap_send, swap_recv, rows_send, rows_recv, local,
):
    place = Place(repeat, groups)
    tok, dim = d_mid.shape
    ff = grad_ff2.shape[0]
    unit_rows = dim // 32
    half = 4 * tok
    role = 2 * place.x + place.y
    loads = [
        pltpu.make_async_copy(grad_o2, grad2, local.at[0]),
        pltpu.make_async_copy(grad_ff2_in, grad_ff2, local.at[1]),
    ]
    for load in loads:
        load.start()
    place.greet()
    sibling = place.member(place.x, 1 - place.core, place.y)

    def stretch(slot, core):
        return d_window.at[slot].at[rows_at(half * core, half)]

    def near(at):
        ref = stretch(2 * place.core, 1 - place.core) if at == 0 else stretch(1, 1 - place.core)
        return remote(ref, near_land.at[at], near_send.at[at], near_recv.at[at], sibling)

    solo = remote(
        stretch(2 * place.core, place.core), side_land.at[place.core], side_send.at[place.core],
        side_recv.at[place.core], place.beside(2 * place.core - 1),
    )
    shared = remote(
        joint, side_land.at[1 - place.core], side_send.at[1 - place.core], side_recv.at[1 - place.core],
        place.beside(1 - 2 * place.core),
    )
    near(0).start()
    solo.start()
    near(1).start()
    cuts = matrices(dim, ff)
    scatters = {
        name: Scatter(place, grad2, 2 * unit_rows, first, width, RS_PLAN[name], True) for name, first, width in cuts
    }
    scatters["ff2"] = Scatter(place, grad_ff2, ff // 16, 0, dim, RS_PLAN["ff2"], False)
    loads[0].wait()
    loads[1].wait()
    near(0).wait_recv()
    joint[...] = (
        d_window[2 - 2 * place.core, rows_at(half * place.core, half)].astype(F32) + near_land[0].astype(F32)
    ).astype(BF16)
    shared.start()
    scatters["ff2"].begin(land_ff2, grad_send.at[2], grad_recv.at[2])
    scatters["ff1"].begin(land_ff1, grad_send.at[1], grad_recv.at[1])
    scatters["out"].begin(land_out, grad_send.at[0], grad_recv.at[0])
    for phase in range(SPLIT):
        for name in REST:
            scatters[name].step(phase)
    near(1).wait_recv()
    own = d_window[1, rows_at(half * place.core, half)].astype(F32) + near_land[1].astype(F32)
    for at in range(2):
        remote(joint, side_land.at[at], side_send.at[at], side_recv.at[at], sibling).wait_recv()
    joined[:, QW:] = (own + side_land[0].astype(F32) + side_land[1].astype(F32)).astype(BF16)
    joined[:, :QW] = d_query[...]
    for at in range(4):
        part = slice(at * tok, (at + 1) * tok)
        partial[part, :] = nt(joined[part, :], heads[...]).astype(BF16)
    to_tokens(place, partial, parts, part_send, part_recv)
    whole = tn(rows[...], joined[...])
    for unit in range(32):
        block = whole[unit * unit_rows:(unit + 1) * unit_rows]
        pad = jnp.zeros((blocks.shape[1] - unit_rows, PW), F32)
        blocks[unit] = jnp.concatenate([block, pad], axis=0).astype(BF16)
    until = 3 if repeat == 1 else 5
    by_heads = ScatterBlocks(place, blocks, RS_HEADS, until)
    by_heads.begin(land_blocks, block_send, block_recv)
    sums = column_sum(joined[...])
    rows_mine[0] = sum_rows[...]
    for row, first in ((4, 0), (5, PW - HW)):
        line = [jnp.where(role == chip, sums[:, first:first + HW], 0.0) for chip in range(CHIPS)]
        rows_mine[0, row:row + 1, :] = jnp.concatenate(line, axis=1)

    def rows_copy(phase):
        return remote(
            rows_mine.at[phase], rows_land.at[phase], rows_send.at[phase], rows_recv.at[phase],
            place.partner(RS_HEADS[phase]),
        )

    def rows_add(phase):
        rows_copy(phase).wait_recv()
        rows_mine[phase + 1] = rows_mine[phase] + rows_land[phase]
        if phase < 4:
            rows_copy(phase + 1).start()

    rows_copy(0).start()
    by_heads.step(0)
    rows_add(0)
    by_heads.step(1)
    rows_add(1)
    for phase in range(SPLIT, 4):
        for name in REST:
            scatters[name].step(phase)
    by_heads.step(2)
    rows_add(2)

    def role_copy(dx, dy):
        chip, device = plane(place, dx, dy)
        at = 2 * dx + dy
        there = place.unit + dx * 4 * (1 - 2 * place.bit(2)) + dy * (1 - 2 * place.bit(0))
        return remote(blocks.at[there], role_land.at[role], plane_send.at[at], plane_recv.at[at], device)

    if repeat == 1:
        for dx, dy in ((1, 1), (1, 0), (0, 1)):
            role_copy(dx, dy).start()
    else:
        by_heads.step(3)
        by_heads.last()
        role_land[...] = jnp.zeros_like(role_land)
    role_land[role] = blocks[place.unit]
    rows_add(3)

    def swap(at):
        name, first, width = cuts[at]
        part = (slice(None), pl.ds(first // 2, width // 2))
        return remote(swap_out.at[part], swap_in.at[part], swap_send.at[at], swap_recv.at[at], place.partner(0))

    def finish_half(at):
        name, first, width = cuts[at]
        target = (g_out, g_ff1)[at]
        total = scatters[name].last()
        high = place.bit(0) == 1
        keep = jnp.where(high, total[unit_rows:], total[:unit_rows])
        give = jnp.where(high, total[:unit_rows], total[unit_rows:])
        pad = jnp.zeros((swap_out.shape[0] - unit_rows, give.shape[1]), F32)
        swap_out[:, first // 2:(first + width) // 2] = jnp.concatenate([give, pad], axis=0).astype(BF16)
        swap(at).start()
        target[:, rows_at(place.bit(0) * (width // 2), width // 2, 128)] = keep

    def finish_swap(at):
        name, first, width = cuts[at]
        target = (g_out, g_ff1)[at]
        swap(at).wait_recv()
        other = swap_in[:, first // 2:(first + width) // 2].astype(F32)[:unit_rows]
        target[:, rows_at((1 - place.bit(0)) * (width // 2), width // 2, 128)] = other

    for at in (1, 0):
        finish_half(at)
    g_ff2[...] = scatters["ff2"].last()
    rows_add(4)
    g_rows[...] = rows_mine[5]
    to_tokens_wait(place, partial, parts, part_send, part_recv)
    d_tokens[...] = (
        d_mid[...] + (parts[0].astype(F32) + parts[1].astype(F32)) + (parts[2].astype(F32) + parts[3].astype(F32))
    ).astype(BF16)
    for at in (1, 0):
        finish_swap(at)
    if repeat == 1:
        for dx, dy in ((1, 1), (1, 0), (0, 1)):
            role_copy(dx, dy).wait_recv()
    for part, first in ((0, 0), (1, QW), (2, QW + HW)):
        line = [role_land[chip][:unit_rows, first:first + HW].astype(F32) for chip in range(CHIPS)]
        g_qkv[:, part * dim:(part + 1) * dim] = jnp.concatenate(line, axis=1)
    for scatter in scatters.values():
        scatter.finish()
    by_heads.finish()
    if repeat == 1:
        for dx, dy in ((1, 1), (1, 0), (0, 1)):
            role_copy(dx, dy).wait_send()
    for at in range(2):
        swap(at).wait_send()
        near(at).wait_send()
    solo.wait_send()
    shared.wait_send()
    for phase in range(5):
        rows_copy(phase).wait_send()
    to_tokens_drain(place, partial, parts, part_send, part_recv)


SPLIT = 2


def leave(repeat, groups, d_query, d_window, rows, heads, d_mid, sum_rows, grad_o2, grad_ff2):
    tok, dim = d_mid.shape
    ff = grad_ff2.shape[0]
    unit = dim // 32
    slab = 2 * unit
    half = 4 * tok
    wide = -(-unit // 16) * 16
    shape = jax.ShapeDtypeStruct
    vm = pltpu.VMEM
    return pl.pallas_call(
        functools.partial(leave_kernel, repeat, groups),
        out_shape=(
            shape((tok, dim), BF16), shape((unit, 3 * dim), F32), shape((unit, dim), F32), shape((unit, ff), F32),
            shape((ff // 32, dim), F32), shape((16, dim), F32),
        ),
        in_specs=[VM] * 6 + [HBM] * 2,
        out_specs=(VM,) * 6,
        scratch_shapes=[
            vm((dim, dim + ff), BF16), vm((ff, dim), BF16),
            vm((31, slab, dim // 2), BF16), vm((31, slab, ff // 2), BF16), vm((31, ff // 32, dim), BF16),
            vm((32, wide, PW), BF16), vm((31, wide, PW), BF16), vm((CHIPS, wide, PW), BF16),
            vm((2, half, KW), BF16), vm((2, half, KW), BF16), vm((half, KW), BF16), vm((half, PW), BF16),
            vm((half, dim), BF16), vm((CHIPS, tok, dim), BF16),
            vm((wide, (dim + ff) // 2), BF16), vm((wide, (dim + ff) // 2), BF16),
            vm((6, 16, dim), F32), vm((5, 16, dim), F32),
            DMA((3, 31)), DMA((3, 31)), DMA((31,)), DMA((31,)), DMA((4,)), DMA((4,)), DMA((2,)), DMA((2,)), DMA((2,)),
            DMA((2,)), DMA((4,)), DMA((4,)), DMA((2,)), DMA((2,)), DMA((5,)), DMA((5,)), DMA((2,)),
        ],
        compiler_params=pltpu.CompilerParams(collective_id=3, has_side_effects=True, vmem_limit_bytes=VMEM_BYTES),
    )(d_query, d_window, rows, heads, d_mid, sum_rows, grad_o2, grad_ff2)


def settle_kernel(
    repeat, out, d_tokens, g_qkv, g_out, g_ff1, g_ff2, g_rows,
    out_r, d_tokens_r, g_qkv_r, g_out_r, g_ff1_r, g_ff2_r, gains_r, shifts_r, biases_r, hidden_r,
):
    for source, target in (
        (out, out_r), (d_tokens, d_tokens_r), (g_qkv, g_qkv_r), (g_out, g_out_r), (g_ff1, g_ff1_r), (g_ff2, g_ff2_r)
    ):
        target[...] = source[...]
    width = g_rows.shape[1]
    per, hidden = gains_r.shape[1], hidden_r.shape[1]
    unit = div(lax.axis_index("blk") * 2 + lax.axis_index("head"), repeat)
    turned = pltpu.roll(g_rows[0:8, :], rem(width - unit * per, width), 1)
    gains_r[...] = turned[0:2, :per]
    shifts_r[...] = turned[2:4, :per]
    biases_r[...] = turned[4:8, :per]
    lines = g_rows[8:16, :]
    row = lax.broadcasted_iota(jnp.int32, lines.shape, 0)
    mine = jnp.sum(jnp.where(row == div(unit * hidden, width), lines, 0.0), axis=0, keepdims=True)
    turned = pltpu.roll(jnp.broadcast_to(mine, lines.shape), rem(width - rem(unit * hidden, width), width), 1)
    hidden_r[...] = turned[0:1, :hidden]


def settle(repeat, results):
    shape = jax.ShapeDtypeStruct
    per, hidden = results[2].shape[0], results[5].shape[0]
    small = [shape((count, per), F32) for count in (2, 2, 4)] + [shape((1, hidden), F32)]
    return pl.pallas_call(
        functools.partial(settle_kernel, repeat),
        out_shape=[shape(value.shape, value.dtype) for value in results[:6]] + small,
        in_specs=[VM] * 7,
        out_specs=[VM] * 10,
        compiler_params=pltpu.CompilerParams(vmem_limit_bytes=VMEM_BYTES),
    )(*results)


def gather_repeat(value, repeat, axis):
    if repeat == 1:
        return value
    count = repeat // 2
    sets = [list(range(at, at + count)) for at in range(0, lax.axis_size("blk"), count)]
    value = lax.all_gather(value, "head", axis=axis, tiled=True)
    if count == 1:
        return value
    return lax.all_gather(value, "blk", axis=axis, tiled=True, axis_index_groups=sets)


def own_share(value, repeat, axis):
    if repeat == 1:
        return value
    count = repeat // 2
    sets = [list(range(at, at + count)) for at in range(0, lax.axis_size("blk"), count)]
    value = lax.psum(value, "head")
    if count > 1:
        value = lax.psum(value, "blk", axis_index_groups=sets)
    size = value.shape[axis] // repeat
    at = jnp.mod(lax.axis_index("blk") * 2 + lax.axis_index("head"), repeat)
    return lax.dynamic_slice_in_dim(value, at * size, size, axis)


def body(tokens, w_qkv, w_out, w_ff1, w_ff2, norm_gains, norm_biases, proj_biases, ff_bias, doc_starts, d_out):
    blks = lax.axis_size("blk")
    repeat = blks * 2 // 32
    groups = blks // GROUP
    tok, dim = tokens.shape
    half_rows = 4 * tok
    total_rows = blks * 2 * tok
    shard_qkv = gather_repeat(w_qkv, repeat, 0)
    shard2 = gather_repeat(jnp.concatenate([w_out, w_ff1], axis=1), repeat, 0)
    shard2 = jnp.pad(shard2, ((0, -shard2.shape[0] % 16), (0, 0)))
    shard_ff2 = gather_repeat(w_ff2, repeat, 0)
    small = pack_small(
        gather_repeat(norm_gains, repeat, 1), gather_repeat(norm_biases, repeat, 1),
        gather_repeat(proj_biases, repeat, 1), gather_repeat(ff_bias, repeat, 0),
    )
    all2, all_ff2, params, ffb, queries, window, rows, heads = enter(
        repeat, groups, shard_qkv, shard2, shard_ff2, small, tokens
    )
    window = window.reshape(6 * half_rows, KW)
    context, sums = forward(total_rows, doc_starts, queries, window)
    out, d_mid, grads, grad_o2, grad_ff2, sum_rows = middle(
        repeat, groups, context, tokens, d_out, params, ffb, all2, all_ff2
    )
    d_query, d_window = backward(total_rows, doc_starts, queries, window, context, grads, sums)
    d_tokens, g_qkv, g_out, g_ff1, g_ff2, g_rows = leave(
        repeat, groups, d_query, d_window.reshape(3, 2 * half_rows, KW), rows, heads, d_mid, sum_rows, grad_o2, grad_ff2
    )
    results = settle(repeat, (out, d_tokens, g_qkv, g_out, g_ff1, g_ff2, g_rows))
    axes = (None, None, 0, 0, 0, 0, 1, 1, 1, 0)
    results = list(results[:9]) + [results[9].reshape(-1)]
    return tuple(
        value if axis is None else own_share(value, repeat, axis) for value, axis in zip(results, axes)
    )


def solution(mesh):
    rows, columns, flat = P(("blk", "head"), None), P(None, ("blk", "head")), P(("blk", "head"))
    return jax.shard_map(
        body,
        mesh=mesh,
        in_specs=(rows,) * 5 + (columns,) * 3 + (flat, P(), rows),
        out_specs=(rows,) * 6 + (columns,) * 3 + (flat,),
        check_vma=False,
    )
```

time: 371 us -> 284 us (0.77); the launches traced: 372 us -> 279 us
  Pallas kernels: 347 us -> 275 us
  local copies, waits for them, and re-layouts: 17 us -> 0 us
    pallas_call x1, Pallas kernels: 144 us -> 102 us  [leave(): pl.pallas_call(functools.partial(leave_kernel, repeat, groups), out_shape...]
    pallas_call x1, Pallas kernels: 117 us -> 83.9 us  [enter(): pl.pallas_call(functools.partial(enter_kernel, repeat, groups), out_shape...]
    unnamed x8 -> x0, local copies, waits for them, and re-layouts: 9.06 us -> none
    broadcast_in_dim x4 -> x0, local copies, waits for them, and re-layouts: 5.11 us -> none  [the longest x1 3.82 us: doc_tables(): jnp.broadcast_to(key_ids[:, None], (window, 128))]
    pallas_call x2 -> x3, Pallas kernels: 52.2 us -> 54.5 us  [the longest x1 31.7 us: backward(): pl.pallas_call(functools.partial(backward_kernel, total_rows), out_shape=...]
where the time goes in v2:
time: 284 us; the launch traced here: 279 us
  Pallas kernels  275 us (97%)
  other arithmetic  3.59 us (1%)
    pallas_call x1, Pallas kernels, leave(): pl.pallas_call(functools.partial(leave_kernel, repeat, groups), out_shape...  102 us
    pallas_call x1, Pallas kernels, enter(): pl.pallas_call(functools.partial(enter_kernel, repeat, groups), out_shape...  83.9 us
    pallas_call x1, Pallas kernels, middle(): pl.pallas_call(functools.partial(middle_kernel, repeat, groups), out_shap...  34.3 us
    pallas_call x1, Pallas kernels, backward(): pl.pallas_call(functools.partial(backward_kernel, total_rows), out_shape=...  31.7 us
    pallas_call x1, Pallas kernels, forward(): pl.pallas_call(functools.partial(forward_kernel, total_rows), out_shape=(...  20.2 us

profile of v2, /device:TPU:0, one launch (start us, length us, event | category | flops | bytes accessed | tf_op | source)
XLA Modules:
  0.0 279.0 jit_solution(16736876293482921689)
XLA Ops:
  0.6 0.7 fusion.9
  1.4 1.3 fusion.4.small
  2.6 1.6 fusion.2.shard2
  4.2 83.9 %shard_map.186 = (bf16[768,3840]{1,0:T(8,128)(2,1)}, bf16[3072,768]{1,0:T(8,128)(2,1)}, f32[8,768]{1,0:T(8,128)}, f32[8,3072]{1,0:T(8,128)}, bf16[1024,256]{1,0:...) custom-call(bf16[24,2304]{1,0:T(8,128)(2,1)} %shard_qkv.1, ...), custom_call_target="tpu_custom_call" | custom-call | tf_op jit(solution)/shard_map/pallas_call | solution.py:539
  88.1 20.2 %shard_map.187 = (f32[1024,256]{1,0:T(8,128)}, f32[8,1024]{1,0:T(8,128)}) custom-call(s32[33]{0:T(128)} %starts.3, bf16[1024,256]{1,0:T(8,128)(2,1)} %get-tuple-element.44.queries, bf16[6144,384]{1,0:T(8,128)(2,1)} %bitcast.4), custom_call_target="tpu_custom_call" | custom-call | tf_op jit(solution)/shard_map/pallas_call | solution.py:688
  108.3 34.3 %shard_map.188 = (bf16[256,768]{1,0:T(8,128)(2,1)}, f32[256,768]{1,0:T(8,128)}, bf16[1024,256]{1,0:T(8,128)(2,1)}, bf16[768,3840]{1,0:T(8,128)(2,1)}, bf16[3072,768]{1,0:T(8,128)(2,1)}, /*index=5*/f32[16,768]{1,0:T(8,128)}) custom-call(f32[1024,256]{1,0:T(8,128)} %get-tuple-element.46.context, bf16[256,768]{1,0:T(8,128)(2,1)} %tokens.3, ...), custom_call_target="tpu_custom_call" | custom-call | tf_op jit(solution)/shard_map/pallas_call | solution.py:875
  142.6 31.7 %shard_map.189 = (bf16[1024,256]{1,0:T(8,128)(2,1)}, bf16[6144,384]{1,0:T(8,128)(2,1)}) custom-call(s32[33]{0:T(128)} %starts.3, bf16[1024,256]{1,0:T(8,128)(2,1)} %get-tuple-element.44.queries, bf16[6144,384]{1,0:T(8,128)(2,1)} %bitcast.5, f32[1024,256]{1,0:T(8,128)} %get-tuple-element.46.context, bf16[1024,256]{1,0:T(8,128)(2,1)} %get-tuple-element.52.grads, ...), custom_call_target="tpu_custom_call" | custom-call | tf_op jit(solution)/shard_map/pallas_call | solution.py:760
  174.3 101.9 %shard_map.190 = (bf16[256,768]{1,0:T(8,128)(2,1)}, f32[24,2304]{1,0:T(8,128)}, f32[24,768]{1,0:T(8,128)}, f32[24,3072]{1,0:T(8,128)}, f32[96,768]{1,0:T(8,128)}, /*index=5*/f32[16,768]{1,0:T(8,128)}) custom-call(bf16[1024,256]{1,0:T(8,128)(2,1)} %get-tuple-element.54.d_query, bf16[3,2048,384]{2,1,0:T(8,128)(2,1)} %bitcast.6, ...), custom_call_target="tpu_custom_call" | custom-call | tf_op jit(solution)/shard_map/pallas_call | solution.py:1085
  276.2 2.6 shard_map.191
